TPU v7x, 128 devices: a whole 4x4x4 slice. The times are simulated.
128 devices in a mesh: section: 2 (over y_lo), dp: 64 (over x, y_hi, z, core).
Axes of the slice: x: 4, y: 4 (y_hi: 2, y_lo: 2; y = y_hi * 2 + y_lo), z: 4, core: 2. Of those that a mesh axis runs over, the one named last changes fastest.
Arguments:
- stream: bfloat16 [2, 4, 64, 128, 640], P('section', None, 'dp'), may hold values from -6 to 6
- cotangent: bfloat16 [2, 4, 64, 128, 640], P('section', None, 'dp'), may hold values from -6 to 6
- lengths: int32 [2, 4, 64], P(None, None, 'dp'), may hold values from 32 to 128, as said below
- pieces: int32 [4, 64], P(None, 'dp'), may hold values from 0 to 3
- configs: int32 [4, 4], replicated, may hold values from 1 to 3072, as said below
- gains: bfloat16 [2, 3, 640], P('section'), may hold values from 0.5 to 1.5
- attn_qkv: bfloat16 [2, 640, 1920], P('section'), may hold values from -0.3125 to 0.3125
- attn_out: bfloat16 [2, 640, 640], P('section'), may hold values from -0.625 to 0.625
- ffn_up: bfloat16 [2, 640, 3072], P('section'), may hold values from -0.25 to 0.25
- ffn_down: bfloat16 [2, 3072, 640], P('section'), may hold values from -0.109375 to 0.109375
- cross_proj: bfloat16 [2, 640, 1280], P('section')
Outputs:
- layer_out: bfloat16 [2, 4, 64, 128, 640], P('section', None, 'dp')
- stream_grad: bfloat16 [2, 4, 64, 128, 640], P('section', None, 'dp')
- gain_grad: float32 [2, 3, 640], P('section', None, 'dp')
- qkv_grad: float32 [2, 640, 1920], P('section', 'dp')
- out_grad: float32 [2, 640, 640], P('section', 'dp')
- up_grad: float32 [2, 640, 3072], P('section', 'dp')
- down_grad: float32 [2, 3072, 640], P('section', 'dp')
- cross_grad: float32 [2, 640, 1280], P('section', 'dp')
Inputs may be any that keep to these rules, and one draw needn't show every extreme that they name: `configs`: column 0 is 640 or 512, column 8 or 4, column 2 one, two or three times 1024, column 3 1 or 2. Some piece has 640, 8, 3072 and 2. `lengths`: in every micro-batch, some sentence of each side has all 128 positions live.
All inputs are finite; a program needn't handle non-finite values.
Results may differ from a plain program's by a relative error of at most 0.024.
Values may be sent and summed in bfloat16 or wider, within the bound.
A program may use at most 448 MiB of HBM per device.

v0:
```python
import jax
import jax.numpy as jnp
from jax import lax
from jax.sharding import PartitionSpec as P

HEADS = 8
HEAD_DIM = 80
FF_BLOCK = 1024


EPSILON = 1e-05
NEGATIVE = -1e30


def sent_to_all(x, axis):
    copies = jnp.broadcast_to(x, (lax.axis_size(axis), *x.shape))
    return lax.all_to_all(copies, axis, split_axis=0, concat_axis=0, tiled=True)


def over_copies(x, axis):
    return sent_to_all(x, axis).sum(axis=0)


def passed_along(value, axis, steps):
    count = lax.axis_size(axis)
    first, last = (max(0, -steps), min(count, count - steps))
    return lax.ppermute(value, axis, [(source, source + steps) for source in range(first, last)])


def cut_along(x, dim, devices):
    shape = x.shape
    blocks = x.reshape(*shape[:dim], devices, shape[dim] // devices, *shape[dim + 1 :])
    return jnp.moveaxis(blocks, dim, 0)


def sum_packed(arrays, axis, dims):
    devices = lax.axis_size(axis)
    blocks = [cut_along(a, dim, devices) for a, dim in zip(arrays, dims)]
    lines = jnp.concatenate([b.reshape(devices, -1) for b in blocks], axis=1)
    rows = max(16, -(-lines.shape[1] // 1024) * 8)
    lines = jnp.pad(lines, ((0, 0), (0, rows * 128 - lines.shape[1]))).reshape(-1, 128)
    vector, at, outs = (lax.psum_scatter(lines, axis, tiled=True).reshape(-1), 0, [])
    for b in blocks:
        part = b[0]
        outs.append(vector[at : at + part.size].reshape(part.shape))
        at += part.size
    return tuple(outs)


def project(barrier_operand, weight_matrix):
    return jnp.einsum(
        "ayb,bc->ayc", barrier_operand, weight_matrix, preferred_element_type=jnp.float32
    )


def project_back(incoming_gradient, weight_matrix):
    return jnp.einsum(
        "zhn,rn->zhr", incoming_gradient, weight_matrix, preferred_element_type=jnp.float32
    )


def weight_grad(barrier_operand, incoming_gradient):
    return jnp.einsum(
        "jxy,jxz->yz", barrier_operand, incoming_gradient, preferred_element_type=jnp.float32
    )


def gelu_slope(hidden):
    normal_cdf = 0.5 * (1.0 + lax.erf(hidden * 0.7071067811865476))
    density = jnp.exp(-0.5 * hidden * hidden) * 0.3989422804014327
    return normal_cdf + hidden * density


def layer_norm(values, norm_gain, feat_mask, live_width):
    average = jnp.sum(values * feat_mask, -1, keepdims=True) / live_width
    centred = (values - average) * feat_mask
    spread = jnp.sum(centred * centred, -1, keepdims=True) / live_width
    inverse = lax.rsqrt(spread + EPSILON)
    normed = centred * inverse
    return (normed * norm_gain, normed, inverse)


def norm_back(incoming_gradient, norm_gain, normed, inverse, feat_mask, live_width):
    dnormed = incoming_gradient * norm_gain * feat_mask
    first_mean = jnp.sum(dnormed, -1, keepdims=True) / live_width
    second_moment_mean = jnp.sum(dnormed * normed, -1, keepdims=True) / live_width
    d_values = inverse * (dnormed - (first_mean + normed * second_moment_mean) * feat_mask)
    return (d_values, jnp.sum(incoming_gradient * normed, axis=(0, 1)))


def split_heads(values):
    return values.reshape(values.shape[0], values.shape[1], HEADS, HEAD_DIM)


def scores_of(queries, key_rows, permitted_mask):
    scaled = jnp.einsum(
        "sqhd,skhd->shqk",
        split_heads(queries),
        split_heads(key_rows),
        preferred_element_type=jnp.float32,
    ) * HEAD_DIM ** (-0.5)
    return jnp.where(permitted_mask, scaled, NEGATIVE)


def attend(queries, key_rows, value_rows, permitted_mask):
    scores = scores_of(queries, key_rows, permitted_mask)
    highest = jnp.max(scores, -1, keepdims=True)
    exponent = jnp.exp(scores - highest)
    summed = jnp.sum(exponent, -1, keepdims=True)
    attention = (exponent / summed).astype(jnp.bfloat16)
    blended = jnp.einsum(
        "shqk,skhd->sqhd", attention, split_heads(value_rows), preferred_element_type=jnp.float32
    )
    return (blended.reshape(queries.shape[0], queries.shape[1], -1), highest + jnp.log(summed))


def attend_back(d_blended, queries, key_rows, value_rows, permitted_mask, logsum):
    scores = scores_of(queries, key_rows, permitted_mask)
    attention = jnp.exp(scores - logsum)
    d_heads = split_heads(d_blended)
    d_values = jnp.einsum(
        "shqk,sqhd->skhd",
        attention.astype(jnp.bfloat16),
        d_heads,
        preferred_element_type=jnp.float32,
    )
    d_attention = jnp.einsum(
        "sqhd,skhd->shqk", d_heads, split_heads(value_rows), preferred_element_type=jnp.float32
    )
    d_scores = (
        attention * (d_attention - jnp.sum(attention * d_attention, -1, keepdims=True))
    ).astype(jnp.bfloat16)
    factor = HEAD_DIM ** (-0.5)
    d_queries = (
        jnp.einsum(
            "shqk,skhd->sqhd", d_scores, split_heads(key_rows), preferred_element_type=jnp.float32
        )
        * factor
    )
    d_keys = (
        jnp.einsum(
            "shqk,sqhd->skhd", d_scores, split_heads(queries), preferred_element_type=jnp.float32
        )
        * factor
    )
    return (
        d_queries.reshape(queries.shape),
        d_keys.reshape(key_rows.shape),
        d_values.reshape(key_rows.shape),
    )


def self_forward(inputs, norm_gain, w_qkv, w_out, permitted_mask, meta, rows):
    live_width, feat_mask, head_mask = (meta[0], meta[1], meta[2])
    normed_out, normed, inverse = layer_norm(inputs, norm_gain, feat_mask, live_width)
    barrier_operand = normed_out.astype(jnp.bfloat16)
    triple = project(barrier_operand, w_qkv).astype(jnp.bfloat16)
    queries, key_rows, value_rows = jnp.split(triple, 3, axis=-1)
    blended, logsum = attend(queries, key_rows, value_rows, permitted_mask)
    heads_out = (blended * head_mask).astype(jnp.bfloat16)
    after = inputs + project(heads_out, w_out) * feat_mask * rows
    return (
        after,
        (normed, inverse, barrier_operand, queries, key_rows, value_rows, logsum, heads_out),
    )


def self_backward(d_after, cache, norm_gain, w_qkv, w_out, permitted_mask, meta, rows):
    live_width, feat_mask, head_mask = (meta[0], meta[1], meta[2])
    normed, inverse, barrier_operand, queries, key_rows, value_rows, logsum, heads_out = cache
    d_branch = (d_after * feat_mask * rows).astype(jnp.bfloat16)
    dw_out = weight_grad(heads_out, d_branch)
    d_heads = (project_back(d_branch, w_out) * head_mask).astype(jnp.bfloat16)
    d_queries, d_keys, d_values = attend_back(
        d_heads, queries, key_rows, value_rows, permitted_mask, logsum
    )
    d_triple = jnp.concatenate([d_queries, d_keys, d_values], axis=-1).astype(jnp.bfloat16)
    dw_qkv = weight_grad(barrier_operand, d_triple)
    d_inputs, d_gain = norm_back(
        project_back(d_triple, w_qkv), norm_gain, normed, inverse, feat_mask, live_width
    )
    return (d_after + d_inputs, d_gain, dw_qkv, dw_out)


def feed_forward(inputs, norm_gain, w_up, w_down, meta, rows):
    live_width, feat_mask, unit_mask = (meta[0], meta[1], meta[3])
    normed_out, normed, inverse = layer_norm(inputs, norm_gain, feat_mask, live_width)
    barrier_operand = normed_out.astype(jnp.bfloat16)
    hidden = project(barrier_operand, w_up)
    activated = (jax.nn.gelu(hidden, approximate=False) * unit_mask).astype(jnp.bfloat16)
    after = inputs + project(activated, w_down) * feat_mask * rows
    return (after, (normed, inverse, barrier_operand, hidden, activated))


def feedforward_backward(d_after, cache, norm_gain, w_up, w_down, meta, rows):
    live_width, feat_mask, unit_mask = (meta[0], meta[1], meta[3])
    normed, inverse, barrier_operand, hidden, activated = cache
    d_branch = (d_after * feat_mask * rows).astype(jnp.bfloat16)
    dw_down = weight_grad(activated, d_branch)
    d_hidden = (project_back(d_branch, w_down) * unit_mask * gelu_slope(hidden)).astype(
        jnp.bfloat16
    )
    dw_up = weight_grad(barrier_operand, d_hidden)
    d_inputs, d_gain = norm_back(
        project_back(d_hidden, w_up), norm_gain, normed, inverse, feat_mask, live_width
    )
    return (d_after + d_inputs, d_gain, dw_up, dw_down)


def cross_forward(inputs, norm_gain, w_cross, key_value, permitted_mask, meta, rows):
    live_width, feat_mask, head_mask = (meta[0], meta[1], meta[2])
    model_width = inputs.shape[-1]
    normed_out, normed, inverse = layer_norm(inputs, norm_gain, feat_mask, live_width)
    barrier_operand = normed_out.astype(jnp.bfloat16)
    queries = project(barrier_operand, w_cross[:, :model_width]).astype(jnp.bfloat16)
    key_rows = jnp.concatenate(
        [key_value[0, :, :, :model_width], key_value[1, :, :, :model_width]], axis=1
    )
    value_rows = jnp.concatenate(
        [key_value[0, :, :, model_width:], key_value[1, :, :, model_width:]], axis=1
    )
    blended, logsum = attend(queries, key_rows, value_rows, permitted_mask)
    heads_out = (blended * head_mask).astype(jnp.bfloat16)
    after = inputs + project(heads_out, w_cross[:, model_width:]) * feat_mask * rows
    return (
        after,
        (normed, inverse, barrier_operand, queries, key_rows, value_rows, logsum, heads_out),
    )


def cross_backward(d_after, cache, norm_gain, w_cross, permitted_mask, meta, rows):
    live_width, feat_mask, head_mask = (meta[0], meta[1], meta[2])
    normed, inverse, barrier_operand, queries, key_rows, value_rows, logsum, heads_out = cache
    model_width = d_after.shape[-1]
    d_branch = (d_after * feat_mask * rows).astype(jnp.bfloat16)
    dw_output = weight_grad(heads_out, d_branch)
    d_heads = (project_back(d_branch, w_cross[:, model_width:]) * head_mask).astype(jnp.bfloat16)
    d_queries, d_keys, d_values = attend_back(
        d_heads, queries, key_rows, value_rows, permitted_mask, logsum
    )
    d_queries = d_queries.astype(jnp.bfloat16)
    dw_query = weight_grad(barrier_operand, d_queries)
    d_inputs, d_gain = norm_back(
        project_back(d_queries, w_cross[:, :model_width]),
        norm_gain,
        normed,
        inverse,
        feat_mask,
        live_width,
    )
    half = d_keys.shape[1] // 2
    d_key_value = jnp.stack(
        [
            jnp.concatenate([d_keys[:, :half], d_values[:, :half]], axis=-1),
            jnp.concatenate([d_keys[:, half:], d_values[:, half:]], axis=-1),
        ]
    ).astype(jnp.bfloat16)
    return (d_after + d_inputs, d_gain, jnp.concatenate([dw_query, dw_output], axis=1), d_key_value)


def encoder_forward(inputs, meta, weights):
    norm_gain, w_qkv, w_out, w_up, w_down, w_cross = weights
    live_width, feat_mask = (meta[0], meta[1])
    after_attn, first_cache = self_forward(
        inputs, norm_gain[0], w_qkv, w_out, meta[6], meta, meta[4]
    )
    result, second_cache = feed_forward(after_attn, norm_gain[1], w_up, w_down, meta, meta[4])
    fresh_output, hat_new, inv_new = layer_norm(result, norm_gain[2], feat_mask, live_width)
    old_out, hat_old, inv_old = layer_norm(inputs, norm_gain[2], feat_mask, live_width)
    encoded = jnp.stack([fresh_output, old_out]).astype(jnp.bfloat16)
    key_value = jnp.einsum(
        "jsld,de->jsle", encoded, w_cross, preferred_element_type=jnp.float32
    ).astype(jnp.bfloat16)
    return (
        result,
        key_value,
        (first_cache, second_cache, hat_new, inv_new, hat_old, inv_old, encoded),
    )


def encoder_backward(inputs, incoming_gradient, d_key_value, meta, weights):
    norm_gain, w_qkv, w_out, w_up, w_down, w_cross = weights
    live_width, feat_mask = (meta[0], meta[1])
    result, key_value, saved = encoder_forward(inputs, meta, weights)
    first_cache, second_cache, hat_new, inv_new, hat_old, inv_old, encoded = saved
    dw_cross = jnp.einsum("jsld,jsle->de", encoded, d_key_value, preferred_element_type=jnp.float32)
    d_encoded = jnp.einsum(
        "jsle,de->jsld", d_key_value, w_cross, preferred_element_type=jnp.float32
    )
    d_new, gain_new = norm_back(d_encoded[0], norm_gain[2], hat_new, inv_new, feat_mask, live_width)
    d_old, gain_old = norm_back(d_encoded[1], norm_gain[2], hat_old, inv_old, feat_mask, live_width)
    d_middle, gain_ffn, dw_up, dw_down = feedforward_backward(
        incoming_gradient + d_new, second_cache, norm_gain[1], w_up, w_down, meta, meta[4]
    )
    d_inputs, gain_attn, dw_qkv, dw_out = self_backward(
        d_middle, first_cache, norm_gain[0], w_qkv, w_out, meta[6], meta, meta[4]
    )
    grads = (
        jnp.stack([gain_attn, gain_ffn, gain_new + gain_old]),
        dw_qkv,
        dw_out,
        dw_up,
        dw_down,
        dw_cross,
    )
    return (d_inputs + d_old, grads)


def decoder_forward(inputs, key_value, meta, weights):
    norm_gain, w_qkv, w_out, w_up, w_down, w_cross = weights
    after_self, first_cache = self_forward(
        inputs, norm_gain[0], w_qkv, w_out, meta[7], meta, meta[5]
    )
    after_cross, second_cache = cross_forward(
        after_self, norm_gain[1], w_cross, key_value, meta[8], meta, meta[5]
    )
    result, third_cache = feed_forward(after_cross, norm_gain[2], w_up, w_down, meta, meta[5])
    return (result, (first_cache, second_cache, third_cache))


def decoder_backward(inputs, key_value, incoming_gradient, meta, weights):
    norm_gain, w_qkv, w_out, w_up, w_down, w_cross = weights
    result, caches = decoder_forward(inputs, key_value, meta, weights)
    d_cross_out, gain_ffn, dw_up, dw_down = feedforward_backward(
        incoming_gradient, caches[2], norm_gain[2], w_up, w_down, meta, meta[5]
    )
    d_self_out, gain_cross, dw_cross, d_key_value = cross_backward(
        d_cross_out, caches[1], norm_gain[1], w_cross, meta[8], meta, meta[5]
    )
    d_inputs, gain_self, dw_qkv, dw_out = self_backward(
        d_self_out, caches[0], norm_gain[0], w_qkv, w_out, meta[7], meta, meta[5]
    )
    grads = (jnp.stack([gain_self, gain_cross, gain_ffn]), dw_qkv, dw_out, dw_up, dw_down, dw_cross)
    return (d_inputs, grads, d_key_value)


def sub_net(chosen, lengths, micro_index, model_width, hidden_width, length):
    feature = jnp.arange(model_width, dtype=jnp.int32)
    places = jnp.arange(length, dtype=jnp.int32)
    key_slots = jnp.arange(2 * length, dtype=jnp.int32)
    picked = chosen[micro_index]
    live_width = picked[:, 0].astype(jnp.float32)[:, None, None]
    feat_mask = (feature[None, None, :] < picked[:, 0, None, None]).astype(jnp.float32)
    head_mask = ((feature // HEAD_DIM)[None, None, :] < picked[:, 1, None, None]).astype(
        jnp.float32
    )
    unit_mask = (
        jnp.arange(hidden_width, dtype=jnp.int32)[None, None, :] < picked[:, 2, None, None]
    ).astype(jnp.float32)
    source = lengths[0, micro_index]
    target = lengths[1, micro_index]
    src_rows = (places[None, :] < source[:, None]).astype(jnp.float32)[:, :, None]
    tgt_rows = (places[None, :] < target[:, None]).astype(jnp.float32)[:, :, None]
    enc_allowed = places[None, None, None, :] < source[:, None, None, None]
    dec_allowed = (places[None, None, None, :] <= places[None, None, :, None]) & (
        places[None, None, None, :] < target[:, None, None, None]
    )
    cross_allowed = ((key_slots % length)[None, None, None, :] < source[:, None, None, None]) & (
        (key_slots // length)[None, None, None, :] < picked[:, 3, None, None, None]
    )
    return (
        live_width,
        feat_mask,
        head_mask,
        unit_mask,
        src_rows,
        tgt_rows,
        enc_allowed,
        dec_allowed,
        cross_allowed,
    )


def shards(
    stream,
    cotangent,
    lengths,
    pieces,
    configs,
    gains,
    attn_qkv,
    attn_out,
    ffn_up,
    ffn_down,
    cross_proj,
):
    micro_count, seq_count, length, model_width = (
        stream.shape[1],
        stream.shape[2],
        stream.shape[3],
        stream.shape[4],
    )
    hidden_width = ffn_up.shape[2]
    later = lax.axis_index("section") == 1
    weights = (
        gains[0].astype(jnp.float32),
        attn_qkv[0],
        attn_out[0],
        ffn_up[0],
        ffn_down[0],
        cross_proj[0],
    )
    onehot = (
        pieces[:, :, None] == jnp.arange(configs.shape[0], dtype=jnp.int32)[None, None, :]
    ).astype(jnp.int32)
    chosen = jnp.sum(onehot[:, :, :, None] * configs[None, None, :, :], axis=2)
    own = jnp.where(later, lengths[1], lengths[0])
    heads_full = (chosen[:, :, 1] == HEADS).astype(jnp.int32)
    wide_two = (chosen[:, :, 2] > FF_BLOCK).astype(jnp.int32)
    wide_three = (chosen[:, :, 2] > 2 * FF_BLOCK).astype(jnp.int32)
    counts = jnp.stack(
        [
            jnp.sum(own),
            jnp.sum(own * heads_full),
            jnp.sum(own * wide_two),
            jnp.sum(own * wide_three),
        ]
    )
    counts = over_copies(counts, "dp")
    metas = [
        sub_net(chosen, lengths, micro_index, model_width, hidden_width, length)
        for micro_index in range(micro_count)
    ]
    zero_kv = jnp.zeros((2, seq_count, length, 2 * model_width), jnp.bfloat16)
    outputs = []
    received = []
    for micro_index in range(micro_count):
        inputs = stream[0, micro_index].astype(jnp.float32)
        meta = metas[micro_index]
        first = lax.cond(
            later,
            lambda: (jnp.zeros_like(inputs), zero_kv),
            lambda: encoder_forward(inputs, meta, weights)[:2],
        )
        arrived = passed_along(first[1], "section", 1)
        received.append(arrived)
        layer_result = lax.cond(
            later, lambda: decoder_forward(inputs, arrived, meta, weights)[0], lambda: first[0]
        )
        outputs.append(layer_result.astype(jnp.bfloat16))
    zero_grads = (
        jnp.zeros((3, model_width), jnp.float32),
        jnp.zeros(attn_qkv.shape[1:], jnp.float32),
        jnp.zeros(attn_out.shape[1:], jnp.float32),
        jnp.zeros(ffn_up.shape[1:], jnp.float32),
        jnp.zeros(ffn_down.shape[1:], jnp.float32),
        jnp.zeros(cross_proj.shape[1:], jnp.float32),
    )
    totals = zero_grads
    shards_total = None
    input_grads = [None] * micro_count
    for micro_index in reversed(range(micro_count)):
        inputs = stream[0, micro_index].astype(jnp.float32)
        incoming_gradient = cotangent[0, micro_index].astype(jnp.float32)
        meta = metas[micro_index]
        arrived = received[micro_index]
        base = totals

        def late_step():
            d_inputs, grads, d_key_value = decoder_backward(
                inputs, arrived, incoming_gradient, meta, weights
            )
            return (d_inputs, jax.tree.map(jnp.add, base, grads), d_key_value)

        def early_step():
            return (jnp.zeros_like(inputs), base, zero_kv)

        first = lax.cond(later, late_step, early_step)
        returned = passed_along(first[2], "section", -1)

        def early_finish():
            d_inputs, grads = encoder_backward(inputs, incoming_gradient, returned, meta, weights)
            return (d_inputs, jax.tree.map(jnp.add, base, grads))

        d_inputs, summed = lax.cond(later, lambda: (first[0], first[1]), early_finish)
        input_grads[micro_index] = d_inputs.astype(jnp.bfloat16)
        totals = summed
    shards_total = sum_packed(
        (totals[0], totals[1], totals[2], totals[3], totals[4], totals[5]), "dp", (1, 0, 0, 0, 0, 0)
    )
    tokens_all = micro_count * seq_count * lax.axis_size("dp") * length
    rates = tokens_all / (counts + tokens_all // 8)
    qkv_cols = jnp.arange(3 * model_width, dtype=jnp.int32) % model_width // HEAD_DIM >= HEADS // 2
    out_count = model_width // lax.axis_size("dp")
    out_rows = (
        lax.axis_index("dp") * out_count + jnp.arange(out_count, dtype=jnp.int32)
    ) // HEAD_DIM >= HEADS // 2
    up_block = jnp.arange(hidden_width, dtype=jnp.int32) // FF_BLOCK
    up_rate = jnp.where(up_block == 0, rates[0], jnp.where(up_block == 1, rates[2], rates[3]))
    down_count = hidden_width // lax.axis_size("dp")
    down_block = (
        lax.axis_index("dp") * down_count + jnp.arange(down_count, dtype=jnp.int32)
    ) // FF_BLOCK
    down_rate = jnp.where(down_block == 0, rates[0], jnp.where(down_block == 1, rates[2], rates[3]))
    layer_out = jnp.stack(outputs)[None]
    stream_grad = jnp.stack(input_grads)[None]
    gain_grad = shards_total[0][None]
    qkv_grad = (shards_total[1] * jnp.where(qkv_cols, rates[1], rates[0])[None, :])[None]
    out_grad = (shards_total[2] * jnp.where(out_rows, rates[1], rates[0])[:, None])[None]
    up_grad = (shards_total[3] * up_rate[None, :])[None]
    down_grad = (shards_total[4] * down_rate[:, None])[None]
    cross_grad = shards_total[5][None]
    return (layer_out, stream_grad, gain_grad, qkv_grad, out_grad, up_grad, down_grad, cross_grad)


def solution(mesh):
    in_specs = (
        P("section", None, "dp", None, None),
        P("section", None, "dp", None, None),
        P(None, None, "dp"),
        P(None, "dp"),
        P(),
        P("section", None, None),
        P("section", None, None),
        P("section", None, None),
        P("section", None, None),
        P("section", None, None),
        P("section", None, None),
    )
    out_specs = (
        P("section", None, "dp", None, None),
        P("section", None, "dp", None, None),
        P("section", None, "dp"),
        P("section", "dp", None),
        P("section", "dp", None),
        P("section", "dp", None),
        P("section", "dp", None),
        P("section", "dp", None),
    )
    return jax.shard_map(shards, mesh=mesh, in_specs=in_specs, out_specs=out_specs, check_vma=False)
```

profile of v0, /device:TPU:0, one launch (start us, length us, event | category | flops | bytes accessed | tf_op | source)
XLA Modules:
  0.0 1167.0 jit_solution(7605883929074457724)
XLA Ops:
  17.5 22.9 %conditional.22 = (f32[1,128,640]{2,1,0:T(8,128)}, bf16[2,1,128,1280]{3,2,0,1:T(8,128)(2,1)}) conditional(s32[]{:T(128)} %convert_element_type.1533, (f32[1,1,640]{2,1,0:T(1,128)S(1)}, f32[1,128,640]{2,1,0:T(8,128)}, f32[1,1,1]{2,1,0:T(1,128)}, f32[3,640]{1,0:T(4,128)S(1)}, bf16[640,1920]{1,0:T(8,128)(2,1)}, ...), branch_computations={%region_67.76_spmd, %region_76.77_spmd} | conditional | flops 1940047488 | bytes 30960488 | solution.py:430
  50.8 21.1 %conditional.20 = (f32[1,128,640]{2,1,0:T(8,128)}, bf16[2,1,128,1280]{3,2,0,1:T(8,128)(2,1)}) conditional(s32[]{:T(128)} %convert_element_type.1533, (f32[1,1,640]{2,1,0:T(1,128)}, f32[1,128,640]{2,1,0:T(8,128)S(1)}, f32[1,1,1]{2,1,0:T(1,128)}, f32[3,640]{1,0:T(4,128)S(1)}, bf16[640,1920]{1,0:T(8,128)(2,1)}, ...), branch_computations={%region_45.54_spmd, %region_54.55_spmd} | conditional | flops 1940047488 | bytes 30960488 | solution.py:430
  82.2 18.5 %conditional.18 = (f32[1,128,640]{2,1,0:T(8,128)S(1)}, bf16[2,1,128,1280]{3,2,0,1:T(8,128)(2,1)S(1)}) conditional(s32[]{:T(128)} %convert_element_type.1533, (f32[1,1,640]{2,1,0:T(1,128)}, f32[1,128,640]{2,1,0:T(8,128)S(1)}, f32[1,1,1]{2,1,0:T(1,128)}, f32[3,640]{1,0:T(4,128)S(1)}, bf16[640,1920]{1,0:T(8,128)(2,1)}, ...), branch_computations={%region_23.0_spmd, %region_32.33_spmd} | conditional | flops 1940047488 | bytes 30960488 | solution.py:430
  116.6 19.6 %conditional.24 = (bf16[1,128,640]{2,1,0:T(8,128)(2,1)}, f32[3,640]{1,0:T(4,128)S(1)}, f32[640,1920]{1,0:T(8,128)}, f32[640,640]{1,0:T(8,128)}, f32[640,3072]{1,...) conditional(s32[]{:T(128)} %convert_element_type.1533, ...), branch_computations={%region_89.90_spmd, %region_90.112_spmd} | conditional | flops 4840503296 | bytes 216117952 | solution.py:468
  146.6 9.9 collective-permute-done.4
  156.5 62.2 %conditional.25 = (f32[3,640]{1,0:T(4,128)S(1)}, f32[640,1920]{1,0:T(8,128)}, f32[640,640]{1,0:T(8,128)}, f32[640,3072]{1,0:T(8,128)}, f32[3072,640]{1,0:T(8,128...) conditional(s32[]{:T(128)} %convert_element_type.1533, (f32[1,1,640]{2,1,0:T(1,128)S(1)}, ...), branch_computations={%region_112.134_spmd, %region_134.135_spmd} | conditional | flops 5291606016 | bytes 155109920 | solution.py:475
  218.8 37.1 %conditional.26 = (bf16[1,128,640]{2,1,0:T(8,128)(2,1)}, f32[3,640]{1,0:T(4,128)S(1)}, f32[640,1920]{1,0:T(8,128)}, f32[640,640]{1,0:T(8,128)}, f32[640,3072]{1,...) conditional(s32[]{:T(128)} %convert_element_type.1533, ...), branch_computations={%region_135.136_spmd, %region_136.158_spmd} | conditional | flops 4846895104 | bytes 260680768 | solution.py:468
  261.9 13.9 %collective-permute-done.5 = bf16[2,1,128,1280]{3,2,0,1:T(8,128)(2,1)S(1)} collective-permute-done((bf16[2,1,128,1280]{3,2,0,1:T(8,128)(2,1)}, bf16[2,1,128,1280]{3,2,0,1:T(8,128)(2,1)S(1)}, u32[]{:S(2)}, u32[]{:S(2)}) %collective-permute-start.5) | collective-permute-done | bytes 655392 | tf_op jit(solution)/shard_map/ppermute | solution.py:27
  275.9 75.5 %conditional.27 = (f32[3,640]{1,0:T(4,128)S(1)}, f32[640,1920]{1,0:T(8,128)}, f32[640,640]{1,0:T(8,128)}, f32[640,3072]{1,0:T(8,128)}, f32[3072,640]{1,0:T(8,128...) conditional(s32[]{:T(128)} %convert_element_type.1533, (f32[1,1,640]{2,1,0:T(1,128)}, ...), branch_computations={%region_158.180_spmd, %region_180.181_spmd} | conditional | flops 5323950080 | bytes 190384160 | solution.py:475
  351.4 28.7 %conditional.28 = (bf16[1,128,640]{2,1,0:T(8,128)(2,1)}, f32[3,640]{1,0:T(4,128)S(1)}, f32[640,1920]{1,0:T(8,128)}, f32[640,640]{1,0:T(8,128)}, f32[640,3072]{1,...) conditional(s32[]{:T(128)} %convert_element_type.1533, ...), branch_computations={%region_181.182_spmd, %region_182.204_spmd} | conditional | flops 4846895104 | bytes 314423552 | solution.py:468
  383.6 31.6 %conditional.16 = (f32[1,128,640]{2,1,0:T(8,128)}, bf16[2,1,128,1280]{3,2,0,1:T(8,128)(2,1)}) conditional(s32[]{:T(128)} %convert_element_type.1533, (f32[1,1,640]{2,1,0:T(1,128)S(1)}, f32[1,128,640]{2,1,0:T(8,128)}, f32[1,1,1]{2,1,0:T(1,128)}, f32[3,640]{1,0:T(4,128)S(1)}, bf16[640,1920]{1,0:T(8,128)(2,1)S(1)}, ...), branch_computations={%region_1.10_spmd, %region_10.11_spmd} | conditional | flops 1940047488 | bytes 24407400 | solution.py:430
  422.2 70.7 %conditional.29 = (f32[3,640]{1,0:T(4,128)S(1)}, f32[640,1920]{1,0:T(8,128)}, f32[640,640]{1,0:T(8,128)}, f32[640,3072]{1,0:T(8,128)}, f32[3072,640]{1,0:T(8,128...) conditional(s32[]{:T(128)} %convert_element_type.1533, (f32[1,1,640]{2,1,0:T(1,128)}, ...), branch_computations={%region_204.226_spmd, %region_226.227_spmd} | conditional | flops 5323950080 | bytes 238885024 | solution.py:475
  492.9 31.2 %conditional.30 = (bf16[1,128,640]{2,1,0:T(8,128)(2,1)}, f32[3,640]{1,0:T(4,128)S(1)}, f32[640,1920]{1,0:T(8,128)}, f32[640,640]{1,0:T(8,128)}, f32[640,3072]{1,...) conditional(s32[]{:T(128)} %convert_element_type.1533, ...), branch_computations={%region_227.228_spmd, %region_228.250_spmd} | conditional | flops 4846895104 | bytes 314425632 | solution.py:468
  527.6 14.7 %collective-permute-done.7 = bf16[2,1,128,1280]{3,2,0,1:T(8,128)(2,1)} collective-permute-done((bf16[2,1,128,1280]{3,2,0,1:T(8,128)(2,1)}, bf16[2,1,128,1280]{3,2,0,1:T(8,128)(2,1)}, u32[]{:S(2)}, u32[]{:S(2)}) %collective-permute-start.7) | collective-permute-done | bytes 655392 | tf_op jit(solution)/shard_map/ppermute | solution.py:27
  542.3 105.0 %conditional.31 = (f32[3,640]{1,0:T(4,128)S(1)}, bf16[1,1,128,640]{3,2,1,0:T(8,128)(2,1)}, f32[64,19200]{1,0:T(8,128)}, f32[64,6400]{1,0:T(8,128)}, f32[64,30720...) conditional(s32[]{:T(128)} %convert_element_type.1533, (f32[1,1,640]{2,1,0:T(1,128)S(1)}, ...), branch_computations={%region_250.272_spmd, %region_272.273_spmd} | conditional | flops 5323950080 | bytes 224198976 | solution.py:475
  619.5 11.4 convolution_add_fusion.20
  649.1 17.5 %dynamic-update-slice.1 = f32[64,99870]{1,0:T(8,128)} dynamic-update-slice(f32[64,99870]{1,0:T(8,128)} %dynamic-update-slice, f32[64,19200]{1,0:T(8,128)} %get-tuple-element.1170, s32[]{} %constant.1513, s32[]{} %constant.1514) | dynamic-update-slice | bytes 9830404
  674.1 23.3 %dynamic-update-slice.3 = f32[64,99870]{1,0:T(8,128)} dynamic-update-slice(f32[64,99870]{1,0:T(8,128)} %dynamic-update-slice.2, f32[64,30720]{1,0:T(8,128)} %get-tuple-element.1172, s32[]{} %constant.1513, s32[]{} %constant.1516) | dynamic-update-slice | bytes 15728644
  697.4 23.3 %dynamic-update-slice.4 = f32[64,99870]{1,0:T(8,128)} dynamic-update-slice(f32[64,99870]{1,0:T(8,128)} %dynamic-update-slice.3, f32[64,30720]{1,0:T(8,128)} %get-tuple-element.1173, s32[]{} %constant.1513, s32[]{} %constant.1517) | dynamic-update-slice | bytes 15728644
  720.7 12.0 %dynamic-update-slice.5 = f32[64,99870]{1,0:T(8,128)} dynamic-update-slice(f32[64,99870]{1,0:T(8,128)} %dynamic-update-slice.4, f32[64,12800]{1,0:T(8,128)} %get-tuple-element.1174, s32[]{} %constant.1513, s32[]{} %constant.1518) | dynamic-update-slice | bytes 6553604 | tf_op jit(solution)/shard_map/concatenate | solution.py:39
  732.7 17.1 %pad.4 = f32[64,100352]{1,0:T(8,128)} pad(f32[64,99870]{1,0:T(8,128)} %dynamic-update-slice.5, f32[]{:T(128)} %constant.1329.clone.1), padding=0_0x0_482 | pad | bytes 51256836 | tf_op jit(solution)/shard_map/jit(_pad)/pad | solution.py:41
  749.8 19.4 %reshape.7813 = f32[50176,128]{1,0:T(8,128)} reshape(f32[64,100352]{1,0:T(8,128)} %pad.4) | data formatting | bytes 51380224 | tf_op jit(solution)/shard_map/reshape | solution.py:41
  774.6 14.8 %all-to-all-start = ((s32[64,1,4]{2,1,0:T(1,128)}), s32[64,1,4]{2,1,0:T(1,128)S(1)}, u32[]{:S(2)}, u32[]{:S(2)}) async-start(s32[64,1,4]{2,1,0:T(1,128)} %broadcast_in_dim.701), calls=%async_computation.1 | async-start | bytes 65536 | tf_op jit(solution)/shard_map/all_to_all | solution.py:17
  835.7 315.4 %reduce-scatter.2.cloned.1.call-done = f32[784,128]{1,0:T(8,128)} async-done(((f32[50176,128]{1,0:T(8,128)}), f32[784,128]{1,0:T(8,128)}) %reduce-scatter.2.cloned.1.call-update) | async-done | bytes 401424 | tf_op jit(solution)/shard_map/reduce_scatter | solution.py:42
  (816 shorter events, 623.5 us)
Async XLA Ops:
  7.2 1143.9 %reduce-scatter.2.cloned.1.call-start = ((), (), s32[]{:S(2)}) async-start(), calls=%async_computation.2 | async-start | bytes 26091520 | tf_op jit(solution)/shard_map/reduce_scatter | solution.py:42
  16.1 140.4 %copy-start.300 = (f32[1,1,3072]{2,1,0:T(1,128)}, f32[1,1,3072]{2,1,0:T(1,128)S(1)}, u32[]{:S(2)}) copy-start(f32[1,1,3072]{2,1,0:T(1,128)S(1)} %compare_convert_fusion) | copy-start | bytes 36868
  17.4 139.1 %copy-start.285 = (f32[1,1,640]{2,1,0:T(1,128)}, f32[1,1,640]{2,1,0:T(1,128)S(1)}, u32[]{:S(2)}) copy-start(f32[1,1,640]{2,1,0:T(1,128)S(1)} %get-tuple-element.2127) | copy-start | bytes 7684
  17.4 139.1 %copy-start.287 = (f32[1,1,640]{2,1,0:T(1,128)}, f32[1,1,640]{2,1,0:T(1,128)S(1)}, u32[]{:S(2)}) copy-start(f32[1,1,640]{2,1,0:T(1,128)S(1)} %get-tuple-element.2128) | copy-start | bytes 7684
  42.5 74.0 %collective-permute-start.3 = (bf16[2,1,128,1280]{2,3,1,0:T(8,128)(2,1)}, bf16[2,1,128,1280]{2,3,1,0:T(8,128)(2,1)}, u32[]{:S(2)}, u32[]{:S(2)}) collective-permute-start(bf16[2,1,128,1280]{2,3,1,0:T(8,128)(2,1)} %copy.632), channel_id=1, source_target_pairs={{0,64},{1,65},{2,66},{3,67},{4,68},{5,69},{6,70},{7,71},{8,72},{9,... | collective-permute-start | bytes 1966088 | tf_op jit(solution)/shard_map/ppermute | solution.py:27
  50.8 225.1 %copy-start.283 = (f32[1,1,640]{2,1,0:T(1,128)}, f32[1,1,640]{2,1,0:T(1,128)S(1)}, u32[]{:S(2)}) copy-start(f32[1,1,640]{2,1,0:T(1,128)S(1)} %get-tuple-element.2129) | copy-start | bytes 7684
  74.0 144.7 %collective-permute-start.2 = (bf16[2,1,128,1280]{2,3,1,0:T(8,128)(2,1)}, bf16[2,1,128,1280]{2,3,1,0:T(8,128)(2,1)}, u32[]{:S(2)}, u32[]{:S(2)}) collective-permute-start(bf16[2,1,128,1280]{2,3,1,0:T(8,128)(2,1)} %copy.631), channel_id=1, source_target_pairs={{0,64},{1,65},{2,66},{3,67},{4,68},{5,69},{6,70},{7,71},{8,72},{9,... | collective-permute-start | bytes 1966088 | tf_op jit(solution)/shard_map/ppermute | solution.py:27
  104.7 246.7 %collective-permute-start.1 = (bf16[2,1,128,1280]{2,3,1,0:T(8,128)(2,1)}, bf16[2,1,128,1280]{2,3,1,0:T(8,128)(2,1)}, u32[]{:S(2)}, u32[]{:S(2)}) collective-permute-start(bf16[2,1,128,1280]{2,3,1,0:T(8,128)(2,1)} %copy.630), channel_id=1, source_target_pairs={{0,64},{1,65},{2,66},{3,67},{4,68},{5,69},{6,70},{7,71},{8,72},{9,... | collective-permute-start | bytes 1966088 | tf_op jit(solution)/shard_map/ppermute | solution.py:27
  110.0 108.8 %copy-start.294 = (f32[1,128,1]{1,2,0:T(1,128)}, f32[1,128,1]{1,2,0:T(1,128)S(1)}, u32[]{:S(2)}) copy-start(f32[1,128,1]{1,2,0:T(1,128)S(1)} %compare_convert_fusion.14) | copy-start | bytes 1540
  138.4 18.2 %collective-permute-start.4 = (bf16[2,1,128,1280]{3,2,0,1:T(8,128)(2,1)}, bf16[2,1,128,1280]{3,2,0,1:T(8,128)(2,1)S(1)}, u32[]{:S(2)}, u32[]{:S(2)}) collective-permute-start(bf16[2,1,128,1280]{3,2,0,1:T(8,128)(2,1)} %copy.633), channel_id=1, source_target_pairs={{64,0},{65,1},{66,2},{67,3},{68,4},{69,5},{70,6},{71,7},{72,8},{73... | collective-permute-start | bytes 1966088 | tf_op jit(solution)/shard_map/ppermute | solution.py:27
  144.0 207.4 %copy-start.304 = (pred[1,1,1,256]{3,2,1,0:T(4,128)(4,1)}, pred[1,1,1,256]{3,2,1,0:T(4,128)(4,1)S(1)}, u32[]{:S(2)}) copy-start(pred[1,1,1,256]{3,2,1,0:T(4,128)(4,1)S(1)} %compare_and_fusion.2) | copy-start | bytes 772
  146.6 72.2 %copy-start.275 = (pred[1,1,128,128]{2,3,1,0:T(8,128)(4,1)}, pred[1,1,128,128]{2,3,1,0:T(8,128)(4,1)S(1)}, u32[]{:S(2)}) copy-start(pred[1,1,128,128]{2,3,1,0:T(8,128)(4,1)S(1)} %fusion.2070) | copy-start | bytes 49156
  258.0 17.8 %collective-permute-start.5 = (bf16[2,1,128,1280]{3,2,0,1:T(8,128)(2,1)}, bf16[2,1,128,1280]{3,2,0,1:T(8,128)(2,1)S(1)}, u32[]{:S(2)}, u32[]{:S(2)}) collective-permute-start(bf16[2,1,128,1280]{3,2,0,1:T(8,128)(2,1)} %copy.637), channel_id=1, source_target_pairs={{64,0},{65,1},{66,2},{67,3},{68,4},{69,5},{70,6},{71,7},{72,8},{73... | collective-permute-start | bytes 1966088 | tf_op jit(solution)/shard_map/ppermute | solution.py:27
  260.7 90.7 %copy-start.277 = (pred[1,1,128,128]{2,3,1,0:T(8,128)(4,1)}, pred[1,1,128,128]{2,3,1,0:T(8,128)(4,1)S(1)}, u32[]{:S(2)}) copy-start(pred[1,1,128,128]{2,3,1,0:T(8,128)(4,1)S(1)} %fusion.2071) | copy-start | bytes 49156
  275.9 75.5 %copy-start.292 = (f32[1,128,1]{1,2,0:T(1,128)S(1)}, f32[1,128,1]{1,2,0:T(1,128)}, u32[]{:S(2)}) copy-start(f32[1,128,1]{1,2,0:T(1,128)} %compare_convert_fusion.16) | copy-start | bytes 1540
  382.3 39.9 %collective-permute-start.6 = (bf16[2,1,128,1280]{3,2,0,1:T(8,128)(2,1)}, bf16[2,1,128,1280]{3,2,0,1:T(8,128)(2,1)}, u32[]{:S(2)}, u32[]{:S(2)}) collective-permute-start(bf16[2,1,128,1280]{3,2,0,1:T(8,128)(2,1)} %copy.641), channel_id=1, source_target_pairs={{64,0},{65,1},{66,2},{67,3},{68,4},{69,5},{70,6},{71,7},{72,8},{73... | collective-permute-start | bytes 1966088 | tf_op jit(solution)/shard_map/ppermute | solution.py:27
  417.4 75.5 %collective-permute-start = (bf16[2,1,128,1280]{2,3,1,0:T(8,128)(2,1)}, bf16[2,1,128,1280]{2,3,1,0:T(8,128)(2,1)}, u32[]{:S(2)}, u32[]{:S(2)}) collective-permute-start(bf16[2,1,128,1280]{2,3,1,0:T(8,128)(2,1)} %copy.629), channel_id=1, source_target_pairs={{0,64},{1,65},{2,66},{3,67},{4,68},{5,69},{6,70},{7,71},{8,72},{9,... | collective-permute-start | bytes 1966088 | tf_op jit(solution)/shard_map/ppermute | solution.py:27
  420.8 72.1 %copy-start.298 = (f32[1,128,1]{1,2,0:T(1,128)}, f32[1,128,1]{1,2,0:T(1,128)S(1)}, u32[]{:S(2)}) copy-start(f32[1,128,1]{1,2,0:T(1,128)S(1)} %compare_convert_fusion.18) | copy-start | bytes 1540
  422.1 70.8 %copy-start.308 = (pred[1,1,1,256]{3,2,1,0:T(4,128)(4,1)}, pred[1,1,1,256]{3,2,1,0:T(4,128)(4,1)S(1)}, u32[]{:S(2)}) copy-start(pred[1,1,1,256]{3,2,1,0:T(4,128)(4,1)S(1)} %compare_and_fusion.3) | copy-start | bytes 772
  422.2 70.7 %copy-start.279 = (pred[1,1,128,128]{2,3,1,0:T(8,128)(4,1)}, pred[1,1,128,128]{2,3,1,0:T(8,128)(4,1)S(1)}, u32[]{:S(2)}) copy-start(pred[1,1,128,128]{2,3,1,0:T(8,128)(4,1)S(1)} %fusion.2072) | copy-start | bytes 49156
  526.3 16.0 %collective-permute-start.7 = (bf16[2,1,128,1280]{3,2,0,1:T(8,128)(2,1)}, bf16[2,1,128,1280]{3,2,0,1:T(8,128)(2,1)}, u32[]{:S(2)}, u32[]{:S(2)}) collective-permute-start(bf16[2,1,128,1280]{3,2,0,1:T(8,128)(2,1)} %copy.645), channel_id=1, source_target_pairs={{64,0},{65,1},{66,2},{67,3},{68,4},{69,5},{70,6},{71,7},{72,8},{73... | collective-permute-start | bytes 1966088 | tf_op jit(solution)/shard_map/ppermute | solution.py:27
  774.6 24.2 %all-to-all-start = ((s32[64,1,4]{2,1,0:T(1,128)}), s32[64,1,4]{2,1,0:T(1,128)S(1)}, u32[]{:S(2)}, u32[]{:S(2)}) async-start(s32[64,1,4]{2,1,0:T(1,128)} %broadcast_in_dim.701), calls=%async_computation.1 | async-start | bytes 65536 | tf_op jit(solution)/shard_map/all_to_all | solution.py:17
  833.6 324.2 %copy-start.329 = (f32[10]{0:T(128)S(1)}, f32[10]{0:T(128)}, u32[]{:S(2)}) copy-start(f32[10]{0:T(128)} %compare_select_fusion.2) | copy-start | bytes 124
  833.6 325.6 %copy-start.321 = (f32[48]{0:T(128)S(1)}, f32[48]{0:T(128)}, u32[]{:S(2)}) copy-start(f32[48]{0:T(128)} %compare_select_fusion.1) | copy-start | bytes 580
  (149 other events, 1032.4 us)
Sparse Core Ops, SparseCore 0:
  769.4 381.6 reduce-scatter.1
where the time goes:
time: 1180 us; the launch traced here: 1170 us
  waiting for transfers between devices  363 us (31%)
  local copies, waits for them, and re-layouts  318 us (27%)
  matrix products  279 us (24%)
  other arithmetic  107 us (9%)
  loops' own time  53.6 us (5%)
  starting transfers between devices  28.5 us (2%)
  between operations  17.7 us (2%)
    reduce_scatter x1, waiting for transfers between devices, sum_packed(): lax.psum_scatter(lines, axis, tiled=True).reshape(-1)  315 us
    dot_general x28, matrix products, project(): jnp.einsum('ayb,bc->ayc', barrier_operand, weight_matrix, preferred_eleme...  91.7 us
    dot_general x16, matrix products, weight_grad(): jnp.einsum('jxy,jxz->yz', barrier_operand, incoming_gradient, preferred_e...  88 us
    unnamed x93, local copies, waits for them, and re-layouts  75.8 us
    cond x253, local copies, waits for them, and re-layouts  65.2 us
    ppermute x8, waiting for transfers between devices, passed_along(): lax.ppermute(value, axis, [(source, source + steps) for source in range(f...  38.6 us
    another operation x4, loops' own time, shards(): first = lax.cond(later, late_step, early_step)  29.1 us
    another operation x5, local copies, waits for them, and re-layouts, sum_packed(): lines = jnp.concatenate([b.reshape(devices, -1) for b in blocks], axis=1)  28.8 us
  transfers between devices with their start and end apart: 10, of which 5 were waited for; matrix products, arithmetic and copies ran while one was open for 32% of the time, Pallas kernels for 0%

commit v1 on v0

v1 whole, which is shorter than its diff:
```python
import jax
import jax.numpy as jnp
from jax import lax
from jax.experimental import pallas as pl
from jax.experimental.pallas import tpu as pltpu
from jax.sharding import PartitionSpec as P

HEADS = 8
HEAD_DIM = 80
FF_BLOCK = 1024


EPSILON = 1e-05
NEGATIVE = -1e30


MESH = pl.DeviceIdType.MESH
NX_AXIS, NY_AXIS, NZ_AXIS, CORES = 4, 2, 4, 2


def place():
    me = lax.axis_index("dp")
    core = me % CORES
    z = me // CORES % NZ_AXIS
    y = me // (CORES * NZ_AXIS) % NY_AXIS
    x = me // (CORES * NZ_AXIS * NY_AXIS)
    return x, y, z, core


def device_at(x, y, z, core):
    return {"dp": ((x * NY_AXIS + y) * NZ_AXIS + z) * CORES + core}


def relative_order(first):
    x, y, z, core = place()
    spot = jnp.arange(640, dtype=jnp.int32)
    rc, ra, rb, ry, t = spot // 320, spot // 80 % 4, spot // 20 % 4, spot // 10 % 2, spot % 10
    rx, rz = (ra, rb) if first == "x" else (rb, ra)
    cx, cy, cz, cc = (x + rx) % 4, (y + ry) % 2, (z + rz) % 4, (core + rc) % 2
    return (((cx * 2 + cy) * 4 + cz) * 2 + cc) * 10 + t


class Sems:
    def __init__(self, send, recv):
        self.send, self.recv, self.at = send, recv, 0

    def copy(self, src, dst, device):
        k = self.at
        self.at += 1
        return pltpu.make_async_remote_copy(
            src_ref=src, dst_ref=dst, send_sem=self.send.at[k], recv_sem=self.recv.at[k],
            device_id=device, device_id_type=MESH)


def add_rows(dst, src, rows, step=16):
    def body(k, _):
        at = pl.ds(pl.multiple_of(k * step, step), step)
        dst[at] = dst[at] + src[at]
        return 0
    lax.fori_loop(0, rows // step, body, 0)


def ring_start(sems, s, buf_a, buf_b, cut, rows, plus, minus):
    a_p = sems.copy(s.at[2, pl.ds(0, cut)], buf_a.at[0, pl.ds(0, cut)], plus)
    a_m = sems.copy(s.at[2, pl.ds(cut, rows - cut)], buf_a.at[1, pl.ds(cut, rows - cut)], minus)
    a_p.start()
    a_m.start()
    b_p = sems.copy(s.at[1, pl.ds(cut, rows - cut)], buf_b.at[0, pl.ds(cut, rows - cut)], plus)
    b_m = sems.copy(s.at[3, pl.ds(0, cut)], buf_b.at[1, pl.ds(0, cut)], minus)
    b_p.start()
    b_m.start()
    return a_p, a_m, b_p, b_m


def ring_middle(sems, copies, s, buf_a, buf_b, cut, rows, plus, minus):
    a_p, a_m, b_p, b_m = copies
    a_p.wait_recv()
    add_rows(s.at[1, pl.ds(0, cut)], buf_a.at[0, pl.ds(0, cut)], cut)
    c_p = sems.copy(s.at[1, pl.ds(0, cut)], buf_b.at[0, pl.ds(0, cut)], plus)
    c_p.start()
    a_m.wait_recv()
    add_rows(s.at[3, pl.ds(cut, rows - cut)], buf_a.at[1, pl.ds(cut, rows - cut)], rows - cut)
    c_m = sems.copy(s.at[3, pl.ds(cut, rows - cut)], buf_b.at[1, pl.ds(cut, rows - cut)], minus)
    c_m.start()
    return c_p, c_m


def ring_end(copies):
    a_p, a_m, b_p, b_m, c_p, c_m = copies
    for c in (b_p, b_m, c_p, c_m):
        c.wait_recv()


def ring_sent(copies):
    for c in copies:
        c.wait_send()


def rs_kernel(fx, fz, dn, ox, oz, od,
              sx, rx, ax, bx, tx, ax2, bx2, yx,
              sz, rz, az, bz, tz, az2, bz2, yz,
              sd, rd, ad, bd, ad2, bd2, yd,
              load_sem, send_sem, recv_sem):
    x, y, z, core = place()
    sib = device_at(x, y, z, 1 - core)
    xp, xm = device_at((x + 1) % 4, y, z, core), device_at((x + 3) % 4, y, z, core)
    zp, zm = device_at(x, y, (z + 1) % 4, core), device_at(x, y, (z + 3) % 4, core)
    yo = device_at(x, 1 - y, z, core)
    barrier = pltpu.get_barrier_semaphore()
    for d in (sib, xp, xm, zp, zm, yo):
        pl.semaphore_signal(barrier, inc=1, device_id=d, device_id_type=MESH)
    loads = []
    order = (2, 1, 3, 0)
    for r in order:
        pair = []
        for k, (src, dst) in enumerate(((fx.at[0, r], sx.at[r]), (fz.at[0, r], sz.at[r]),
                         (dn.at[:, :, (z + r) % 4, core], sd.at[r]))):
            c = pltpu.make_async_copy(src, dst, load_sem.at[r * 3 + k])
            c.start()
            pair.append(c)
        loads.append(pair)
    pl.semaphore_wait(barrier, 6)
    sems = Sems(send_sem, recv_sem)
    cores = []
    for r in order:
        pair = []
        for src, dst in ((fx.at[1, r], rx.at[r]), (fz.at[1, r], rz.at[r]),
                         (dn.at[:, :, (z + r) % 4, 1 - core], rd.at[r])):
            c = sems.copy(src, dst, sib)
            c.start()
            pair.append(c)
        cores.append(pair)

    def summed(k):
        r = order[k]
        for j, (s, got) in enumerate(((sx, rx), (sz, rz), (sd, rd))):
            loads[k][j].wait()
            cores[k][j].wait_recv()
            if j == 2:
                def body(i, _):
                    s[r, i // 2, i % 2] = s[r, i // 2, i % 2] + got[r, i // 2, i % 2]
                    return 0
                lax.fori_loop(0, 8, body, 0)
            else:
                add_rows(s.at[r], got.at[r], s.shape[1])

    rows_x, cut_x = 80, 48
    def d_copy(src, dst, lo, dev):
        return sems.copy(src.at[pl.ds(lo, 2)], dst.at[pl.ds(lo, 2)], dev)

    def d_add(dst, got, lo):
        def body(i, _):
            a, b = lo + i // 2, i % 2
            dst[a, b] = dst[a, b] + got[a, b]
            return 0
        lax.fori_loop(0, 4, body, 0)

    summed(0)
    a = []
    a.append((sems.copy(sx.at[2, pl.ds(0, 48)], ax.at[0, pl.ds(0, 48)], xp), sems.copy(sx.at[2, pl.ds(48, 32)], ax.at[1, pl.ds(48, 32)], xm)))
    a.append((sems.copy(sz.at[2, pl.ds(0, 48)], az.at[0, pl.ds(0, 48)], zp), sems.copy(sz.at[2, pl.ds(48, 32)], az.at[1, pl.ds(48, 32)], zm)))
    a.append((d_copy(sd.at[2], ad.at[0], 0, zp), d_copy(sd.at[2], ad.at[1], 2, zm)))
    for p in a:
        p[0].start(); p[1].start()
    summed(1)
    b = [[sems.copy(sx.at[1, pl.ds(48, 32)], bx.at[0, pl.ds(48, 32)], xp)],
         [sems.copy(sz.at[1, pl.ds(48, 32)], bz.at[0, pl.ds(48, 32)], zp)],
         [d_copy(sd.at[1], bd.at[0], 2, zp)]]
    for p in b:
        p[0].start()
    summed(2)
    b[0].append(sems.copy(sx.at[3, pl.ds(0, 48)], bx.at[1, pl.ds(0, 48)], xm))
    b[1].append(sems.copy(sz.at[3, pl.ds(0, 48)], bz.at[1, pl.ds(0, 48)], zm))
    b[2].append(d_copy(sd.at[3], bd.at[1], 0, zm))
    for p in b:
        p[1].start()
    c = []
    for j, (s, ba, bb, plus, minus) in enumerate(((sx, ax, bx, xp, xm), (sz, az, bz, zp, zm))):
        a[j][0].wait_recv()
        add_rows(s.at[1, pl.ds(0, 48)], ba.at[0, pl.ds(0, 48)], 48)
        cp = sems.copy(s.at[1, pl.ds(0, 48)], bb.at[0, pl.ds(0, 48)], plus)
        cp.start()
        a[j][1].wait_recv()
        add_rows(s.at[3, pl.ds(48, 32)], ba.at[1, pl.ds(48, 32)], 32)
        cm = sems.copy(s.at[3, pl.ds(48, 32)], bb.at[1, pl.ds(48, 32)], minus)
        cm.start()
        c.append((cp, cm))
    a[2][0].wait_recv()
    d_add(sd.at[1], ad.at[0], 0)
    cp = d_copy(sd.at[1], bd.at[0], 0, zp)
    cp.start()
    a[2][1].wait_recv()
    d_add(sd.at[3], ad.at[1], 2)
    cm = d_copy(sd.at[3], bd.at[1], 2, zm)
    cm.start()
    c.append((cp, cm))
    summed(3)

    second = []
    for j, (s, bb, t, ba2, bb2, plus, minus) in enumerate(((sx, bx, tx, ax2, bx2, zp, zm), (sz, bz, tz, az2, bz2, xp, xm))):
        for k in (*b[j], *c[j]):
            k.wait_recv()
        for r in range(4):
            got = (s[0, pl.ds(20 * r, 20)].astype(jnp.float32) + bb[0, pl.ds(20 * r, 20)].astype(jnp.float32) + bb[1, pl.ds(20 * r, 20)].astype(jnp.float32))
            t[r] = jnp.concatenate([got, jnp.zeros((12, got.shape[1]), jnp.float32)], axis=0).astype(jnp.bfloat16)
        second.append(ring_start(sems, t, ba2, bb2, 16, 32, plus, minus))
    for k in (*b[2], *c[2]):
        k.wait_recv()

    def body(i, _):
        p, q = i // 2, i % 2
        sd[0, p, q] = sd[0, p, q] + bd[0, p, q] + bd[1, p, q]
        return 0
    lax.fori_loop(0, 8, body, 0)
    def chunk(r, q):
        return sd.at[0, (x + r) % 4, q]
    dsec = [sems.copy(chunk(2, 0), ad2.at[0], xp), sems.copy(chunk(2, 1), ad2.at[1], xm),
            sems.copy(chunk(1, 1), bd2.at[0, 1], xp), sems.copy(chunk(3, 0), bd2.at[1, 0], xm)]
    for k in dsec:
        k.start()
    third = []
    for j, (t, ba2, bb2, plus, minus) in enumerate(((tx, ax2, bx2, zp, zm), (tz, az2, bz2, xp, xm))):
        third.append(ring_middle(sems, second[j], t, ba2, bb2, 16, 32, plus, minus))
    dsec[0].wait_recv()
    sd[0, (x + 1) % 4, 0] = sd[0, (x + 1) % 4, 0] + ad2[0]
    dc = [sems.copy(chunk(1, 0), bd2.at[0, 0], xp)]
    dc[0].start()
    dsec[1].wait_recv()
    sd[0, (x + 3) % 4, 1] = sd[0, (x + 3) % 4, 1] + ad2[1]
    dc.append(sems.copy(chunk(3, 1), bd2.at[1, 1], xm))
    dc[1].start()
    ys = []
    for j, (t, bb2, yb, o) in enumerate(((tx, bx2, yx, ox), (tz, bz2, yz, oz))):
        ring_end((*second[j], *third[j]))
        f = t[0].astype(jnp.float32) + bb2[0].astype(jnp.float32) + bb2[1].astype(jnp.float32)
        yb[0] = f[10:26].astype(jnp.bfloat16)
        o[...] = f[0:10]
        k = sems.copy(yb.at[0], yb.at[1], yo)
        k.start()
        ys.append(k)
    for k in (dsec[2], dsec[3], *dc):
        k.wait_recv()
    def full(q):
        return (sd[0, x, q].astype(jnp.float32) + bd2[0, q].astype(jnp.float32) + bd2[1, q].astype(jnp.float32))
    yd[0] = full(1 - y).astype(jnp.bfloat16)
    k = sems.copy(yd.at[0], yd.at[1], yo)
    k.start()
    ys.append(k)
    od[...] = full(y)
    for k, yb, o in zip(ys, (yx, yz, yd), (ox, oz, od)):
        k.wait_recv()
        o[...] = o[...] + yb[1][: o.shape[0]].astype(jnp.float32)
    for group in (*cores, *a, *b, *c, *second, *third, dsec, dc, ys):
        ring_sent(group)


def reduce_scatter(fx, fz, dn):
    nx, nz = fx.shape[1], fz.shape[1]
    bf, f32 = jnp.bfloat16, jnp.float32
    V = pltpu.VMEM
    def feature(n):
        return [V((4, 80, n), bf), V((4, 80, n), bf), V((2, 80, n), bf), V((2, 80, n), bf),
                V((4, 32, n), bf), V((2, 32, n), bf), V((2, 32, n), bf), V((2, 16, n), bf)]
    w = dn.shape[1]
    down = [V((4, 4, 2, 48, w), bf), V((4, 4, 2, 48, w), bf), V((2, 4, 2, 48, w), bf), V((2, 4, 2, 48, w), bf),
            V((2, 48, w), bf), V((2, 2, 48, w), bf), V((2, 48, w), bf)]
    return pl.pallas_call(
        rs_kernel,
        out_shape=(jax.ShapeDtypeStruct((10, nx), f32), jax.ShapeDtypeStruct((10, nz), f32), jax.ShapeDtypeStruct((48, w), f32)),
        in_specs=[pl.BlockSpec(memory_space=pl.ANY)] * 3,
        out_specs=[pl.BlockSpec(memory_space=pltpu.VMEM)] * 3,
        scratch_shapes=[*feature(nx), *feature(nz), *down,
                        pltpu.SemaphoreType.DMA((12,)), pltpu.SemaphoreType.DMA((51,)), pltpu.SemaphoreType.DMA((51,))],
        compiler_params=pltpu.CompilerParams(collective_id=0, has_side_effects=True, vmem_limit_bytes=60 * 1024 * 1024),
        name="sum_gradients",
    )(fx.reshape(2, 4, 80, nx), fz.reshape(2, 4, 80, nz), dn.reshape(4, 2, 4, 2, 48, w))


def project(barrier_operand, weight_matrix):
    return jnp.einsum(
        "ayb,bc->ayc", barrier_operand, weight_matrix, preferred_element_type=jnp.float32
    )


def project_back(incoming_gradient, weight_matrix):
    return jnp.einsum(
        "zhn,rn->zhr", incoming_gradient, weight_matrix, preferred_element_type=jnp.float32
    )


def weight_grad(barrier_operand, incoming_gradient):
    return jnp.einsum(
        "jxy,jxz->yz", barrier_operand, incoming_gradient, preferred_element_type=jnp.float32
    )


def gelu_slope(hidden):
    normal_cdf = 0.5 * (1.0 + lax.erf(hidden * 0.7071067811865476))
    density = jnp.exp(-0.5 * hidden * hidden) * 0.3989422804014327
    return normal_cdf + hidden * density


def layer_norm(values, norm_gain, feat_mask, live_width):
    average = jnp.sum(values * feat_mask, -1, keepdims=True) / live_width
    centred = (values - average) * feat_mask
    spread = jnp.sum(centred * centred, -1, keepdims=True) / live_width
    inverse = lax.rsqrt(spread + EPSILON)
    normed = centred * inverse
    return (normed * norm_gain, normed, inverse)


def norm_back(incoming_gradient, norm_gain, normed, inverse, feat_mask, live_width):
    dnormed = incoming_gradient * norm_gain * feat_mask
    first_mean = jnp.sum(dnormed, -1, keepdims=True) / live_width
    second_moment_mean = jnp.sum(dnormed * normed, -1, keepdims=True) / live_width
    d_values = inverse * (dnormed - (first_mean + normed * second_moment_mean) * feat_mask)
    return (d_values, jnp.sum(incoming_gradient * normed, axis=(0, 1)))


def split_heads(values):
    return values.reshape(values.shape[0], values.shape[1], HEADS, HEAD_DIM)


def scores_of(queries, key_rows, permitted_mask):
    scaled = jnp.einsum(
        "sqhd,skhd->shqk",
        split_heads(queries),
        split_heads(key_rows),
        preferred_element_type=jnp.float32,
    ) * HEAD_DIM ** (-0.5)
    return jnp.where(permitted_mask, scaled, NEGATIVE)


def attend(queries, key_rows, value_rows, permitted_mask):
    scores = scores_of(queries, key_rows, permitted_mask)
    highest = jnp.max(scores, -1, keepdims=True)
    exponent = jnp.exp(scores - highest)
    summed = jnp.sum(exponent, -1, keepdims=True)
    attention = (exponent / summed).astype(jnp.bfloat16)
    blended = jnp.einsum(
        "shqk,skhd->sqhd", attention, split_heads(value_rows), preferred_element_type=jnp.float32
    )
    return (blended.reshape(queries.shape[0], queries.shape[1], -1), highest + jnp.log(summed))


def attend_back(d_blended, queries, key_rows, value_rows, permitted_mask, logsum):
    scores = scores_of(queries, key_rows, permitted_mask)
    attention = jnp.exp(scores - logsum)
    d_heads = split_heads(d_blended)
    d_values = jnp.einsum(
        "shqk,sqhd->skhd",
        attention.astype(jnp.bfloat16),
        d_heads,
        preferred_element_type=jnp.float32,
    )
    d_attention = jnp.einsum(
        "sqhd,skhd->shqk", d_heads, split_heads(value_rows), preferred_element_type=jnp.float32
    )
    d_scores = (
        attention * (d_attention - jnp.sum(attention * d_attention, -1, keepdims=True))
    ).astype(jnp.bfloat16)
    factor = HEAD_DIM ** (-0.5)
    d_queries = (
        jnp.einsum(
            "shqk,skhd->sqhd", d_scores, split_heads(key_rows), preferred_element_type=jnp.float32
        )
        * factor
    )
    d_keys = (
        jnp.einsum(
            "shqk,sqhd->skhd", d_scores, split_heads(queries), preferred_element_type=jnp.float32
        )
        * factor
    )
    return (
        d_queries.reshape(queries.shape),
        d_keys.reshape(key_rows.shape),
        d_values.reshape(key_rows.shape),
    )


def self_forward(inputs, norm_gain, w_qkv, w_out, permitted_mask, meta, rows):
    live_width, feat_mask, head_mask = (meta[0], meta[1], meta[2])
    normed_out, normed, inverse = layer_norm(inputs, norm_gain, feat_mask, live_width)
    barrier_operand = normed_out.astype(jnp.bfloat16)
    triple = project(barrier_operand, w_qkv).astype(jnp.bfloat16)
    queries, key_rows, value_rows = jnp.split(triple, 3, axis=-1)
    blended, logsum = attend(queries, key_rows, value_rows, permitted_mask)
    heads_out = (blended * head_mask).astype(jnp.bfloat16)
    after = inputs + project(heads_out, w_out) * feat_mask * rows
    return (
        after,
        (normed, inverse, barrier_operand, queries, key_rows, value_rows, logsum, heads_out),
    )


def self_backward(d_after, cache, norm_gain, w_qkv, w_out, permitted_mask, meta, rows, order_x, order_z):
    live_width, feat_mask, head_mask = (meta[0], meta[1], meta[2])
    normed, inverse, barrier_operand, queries, key_rows, value_rows, logsum, heads_out = cache
    d_branch = (d_after * feat_mask * rows).astype(jnp.bfloat16)
    dw_out = weight_grad16(layer_part(heads_out, order_z), d_branch)
    d_heads = (project_back(d_branch, w_out) * head_mask).astype(jnp.bfloat16)
    d_queries, d_keys, d_values = attend_back(
        d_heads, queries, key_rows, value_rows, permitted_mask, logsum
    )
    d_triple = jnp.concatenate([d_queries, d_keys, d_values], axis=-1).astype(jnp.bfloat16)
    dw_x = weight_grad16(layer_part(barrier_operand, order_x), d_triple[..., :1280])
    dw_z = weight_grad16(layer_part(barrier_operand, order_z), d_triple[..., 1280:])
    d_inputs, d_gain = norm_back(
        project_back(d_triple, w_qkv), norm_gain, normed, inverse, feat_mask, live_width
    )
    return (d_after + d_inputs, d_gain, dw_x, dw_z, dw_out)


def feed_forward(inputs, norm_gain, w_up, w_down, meta, rows):
    live_width, feat_mask, unit_mask = (meta[0], meta[1], meta[3])
    normed_out, normed, inverse = layer_norm(inputs, norm_gain, feat_mask, live_width)
    barrier_operand = normed_out.astype(jnp.bfloat16)
    hidden = project(barrier_operand, w_up)
    activated = (jax.nn.gelu(hidden, approximate=False) * unit_mask).astype(jnp.bfloat16)
    after = inputs + project(activated, w_down) * feat_mask * rows
    return (after, (normed, inverse, barrier_operand, hidden, activated))


def ffn_back(d_after, cache, norm_gain, w_up, w_down, meta, rows, order_x):
    live_width, feat_mask, unit_mask = (meta[0], meta[1], meta[3])
    normed, inverse, barrier_operand, hidden, activated = cache
    d_branch = (d_after * feat_mask * rows).astype(jnp.bfloat16)
    dw_down = weight_grad16(activated, d_branch)
    d_hidden = (project_back(d_branch, w_down) * unit_mask * gelu_slope(hidden)).astype(
        jnp.bfloat16
    )
    dw_up = weight_grad16(layer_part(barrier_operand, order_x), d_hidden)
    d_inputs, d_gain = norm_back(
        project_back(d_hidden, w_up), norm_gain, normed, inverse, feat_mask, live_width
    )
    return (d_after + d_inputs, d_gain, dw_up, dw_down)


def cross_forward(inputs, norm_gain, w_cross, key_value, permitted_mask, meta, rows):
    live_width, feat_mask, head_mask = (meta[0], meta[1], meta[2])
    model_width = inputs.shape[-1]
    normed_out, normed, inverse = layer_norm(inputs, norm_gain, feat_mask, live_width)
    barrier_operand = normed_out.astype(jnp.bfloat16)
    queries = project(barrier_operand, w_cross[:, :model_width]).astype(jnp.bfloat16)
    key_rows = jnp.concatenate(
        [key_value[0, :, :, :model_width], key_value[1, :, :, :model_width]], axis=1
    )
    value_rows = jnp.concatenate(
        [key_value[0, :, :, model_width:], key_value[1, :, :, model_width:]], axis=1
    )
    blended, logsum = attend(queries, key_rows, value_rows, permitted_mask)
    heads_out = (blended * head_mask).astype(jnp.bfloat16)
    after = inputs + project(heads_out, w_cross[:, model_width:]) * feat_mask * rows
    return (
        after,
        (normed, inverse, barrier_operand, queries, key_rows, value_rows, logsum, heads_out),
    )


def cross_backward(d_after, cache, norm_gain, w_cross, permitted_mask, meta, rows, order_x):
    live_width, feat_mask, head_mask = (meta[0], meta[1], meta[2])
    normed, inverse, barrier_operand, queries, key_rows, value_rows, logsum, heads_out = cache
    model_width = d_after.shape[-1]
    d_branch = (d_after * feat_mask * rows).astype(jnp.bfloat16)
    dw_output = weight_grad16(layer_part(heads_out, order_x), d_branch)
    d_heads = (project_back(d_branch, w_cross[:, model_width:]) * head_mask).astype(jnp.bfloat16)
    d_queries, d_keys, d_values = attend_back(
        d_heads, queries, key_rows, value_rows, permitted_mask, logsum
    )
    d_queries = d_queries.astype(jnp.bfloat16)
    dw_query = weight_grad16(layer_part(barrier_operand, order_x), d_queries)
    d_inputs, d_gain = norm_back(
        project_back(d_queries, w_cross[:, :model_width]),
        norm_gain,
        normed,
        inverse,
        feat_mask,
        live_width,
    )
    half = d_keys.shape[1] // 2
    d_key_value = jnp.stack(
        [
            jnp.concatenate([d_keys[:, :half], d_values[:, :half]], axis=-1),
            jnp.concatenate([d_keys[:, half:], d_values[:, half:]], axis=-1),
        ]
    ).astype(jnp.bfloat16)
    return (d_after + d_inputs, d_gain, jnp.concatenate([dw_query, dw_output], axis=1), d_key_value)


def layer_part(values, order):
    picks = (jnp.arange(640, dtype=jnp.int32)[:, None] == order[None, :]).astype(jnp.bfloat16)
    return jnp.einsum("ayb,bc->ayc", values, picks, preferred_element_type=jnp.float32).astype(jnp.bfloat16)


def weight_grad16(operand, gradient):
    return weight_grad(operand, gradient).astype(jnp.bfloat16)


def shards(stream, cotangent, lengths, pieces, configs, gains, attn_qkv, attn_out, ffn_up, ffn_down, cross_proj):
    f32, bf16 = jnp.float32, jnp.bfloat16
    micro, length, width = stream.shape[1], stream.shape[3], stream.shape[4]
    hidden_width = ffn_up.shape[2]
    later = lax.axis_index("section") == 1
    rows_in = stream.reshape(micro, length, width)
    cot = cotangent.reshape(micro, length, width).astype(f32)
    norm_gain = gains[0].astype(f32)
    w_qkv, w_out, w_up, w_down, w_cross = attn_qkv[0], attn_out[0], ffn_up[0], ffn_down[0], cross_proj[0]
    enc_rows = lax.ppermute(rows_in, "section", [(0, 1)])
    enc_gain = lax.ppermute(gains[0, 2:3], "section", [(0, 1)]).astype(f32)[0]
    enc_cross = lax.ppermute(w_cross, "section", [(0, 1)])
    chosen = configs[pieces[:, 0]]
    lens = lengths[:, :, 0]
    own = jnp.where(later, lens[1], lens[0])
    heads_full = (chosen[:, 1] == HEADS).astype(jnp.int32)
    wide_two = (chosen[:, 2] > FF_BLOCK).astype(jnp.int32)
    wide_three = (chosen[:, 2] > 2 * FF_BLOCK).astype(jnp.int32)
    counts = jnp.stack([jnp.sum(own), jnp.sum(own * heads_full), jnp.sum(own * wide_two), jnp.sum(own * wide_three)])
    counts = lax.psum(counts, "dp")

    places = jnp.arange(length, dtype=jnp.int32)
    feature = jnp.arange(width, dtype=jnp.int32)
    live_width = chosen[:, 0].astype(f32)[:, None, None]
    feat_mask = (feature[None, None, :] < chosen[:, 0, None, None]).astype(f32)
    head_mask = ((feature // HEAD_DIM)[None, None, :] < chosen[:, 1, None, None]).astype(f32)
    unit_mask = (jnp.arange(hidden_width, dtype=jnp.int32)[None, None, :] < chosen[:, 2, None, None]).astype(f32)
    rows = (places[None, :] < own[:, None]).astype(f32)[:, :, None]
    self_allowed = (places[None, None, None, :] < own[:, None, None, None]) & (
        (places[None, None, None, :] <= places[None, None, :, None]) | jnp.logical_not(later))
    key_slots = jnp.arange(2 * length, dtype=jnp.int32)
    cross_allowed = ((key_slots % length)[None, None, None, :] < lens[0][:, None, None, None]) & (
        (key_slots // length)[None, None, None, :] < chosen[:, 3, None, None, None])
    meta = (live_width, feat_mask, head_mask, unit_mask)

    x = rows_in.astype(f32)
    x1, self_cache = self_forward(x, norm_gain[0], w_qkv, w_out, self_allowed, meta, rows)

    def enc_a():
        x2, _ = feed_forward(x1, norm_gain[1], w_up, w_down, meta, rows)
        fresh, _, _ = layer_norm(x2, norm_gain[2], feat_mask, live_width)
        return x2, fresh.astype(bf16)

    x2, fresh = lax.cond(later, lambda: (x1, jnp.zeros(rows_in.shape, bf16)), enc_a)
    fresh = lax.ppermute(fresh, "section", [(0, 1)])

    order_x, order_z = relative_order("x"), relative_order("z")

    def dec_b():
        old, _, _ = layer_norm(enc_rows.astype(f32), enc_gain, feat_mask, live_width)
        encoded = jnp.stack([fresh, old.astype(bf16)])
        key_value = jnp.einsum("jsld,de->jsle", encoded, enc_cross, preferred_element_type=f32).astype(bf16)
        y2, cross_cache = cross_forward(x1, norm_gain[1], w_cross, key_value, cross_allowed, meta, rows)
        y3, ffn_cache = feed_forward(y2, norm_gain[2], w_up, w_down, meta, rows)
        d_y2, gain_ffn, d_up, d_down = ffn_back(cot, ffn_cache, norm_gain[2], w_up, w_down, meta, rows, order_x)
        d_y1, gain_cross, d_cross, d_kv = cross_backward(d_y2, cross_cache, norm_gain[1], w_cross, cross_allowed, meta, rows, order_x)
        d_enc = jnp.einsum("jsle,de->jsld", d_kv, enc_cross, preferred_element_type=f32).astype(bf16)
        d_wc = weight_grad16(layer_part(encoded.reshape(-1, length, width), order_z), d_kv.reshape(-1, length, 2 * width))
        return y3, d_y1, gain_cross, gain_ffn, d_up, d_down, d_cross, d_wc, d_enc

    def enc_b():
        z = jnp.zeros
        return (x2, x1, z(width, f32), z(width, f32), z((width, hidden_width), bf16), z((hidden_width, width), bf16),
                z((width, 2 * width), bf16), z((width, 2 * width), bf16), z((2, *rows_in.shape), bf16))

    out, d_y1, gain_b, gain_c, d_up, d_down, d_cross, d_wc, d_enc = lax.cond(later, dec_b, enc_b)
    back = lax.ppermute(d_enc, "section", [(1, 0)])

    def enc_c():
        _, hat_new, inv_new = layer_norm(x2, norm_gain[2], feat_mask, live_width)
        _, hat_old, inv_old = layer_norm(x, norm_gain[2], feat_mask, live_width)
        _, ffn_cache = feed_forward(x1, norm_gain[1], w_up, w_down, meta, rows)
        d_new, gain_new = norm_back(back[0].astype(f32), norm_gain[2], hat_new, inv_new, feat_mask, live_width)
        d_old, gain_old = norm_back(back[1].astype(f32), norm_gain[2], hat_old, inv_old, feat_mask, live_width)
        d_x1, gain_ffn, du, dd = ffn_back(cot + d_new, ffn_cache, norm_gain[1], w_up, w_down, meta, rows, order_x)
        return d_x1, d_old, gain_ffn, gain_new + gain_old, du, dd

    d_x1, d_old, gain_b, gain_c, d_up, d_down = lax.cond(
        later, lambda: (d_y1, jnp.zeros_like(x), gain_b, gain_c, d_up, d_down), enc_c)
    d_in, gain_a, d_qkv_x, d_qkv_z, d_out = self_backward(
        d_x1, self_cache, norm_gain[0], w_qkv, w_out, self_allowed, meta, rows, order_x, order_z)
    d_in = d_in + d_old
    gain_t = jnp.stack([gain_a, gain_b, gain_c])
    picks = (feature[:, None] == order_z[None, :]).astype(f32)
    gain_t = jnp.einsum("gf,fp->pg", gain_t, picks, precision=lax.Precision.HIGHEST).astype(bf16)
    gain_t = jnp.pad(gain_t, ((0, 0), (0, 125)))
    fx = jnp.concatenate([d_up, d_qkv_x, d_cross], axis=1)
    fz = jnp.concatenate([d_out, d_qkv_z, gain_t, d_wc], axis=1)
    ox, oz, od = reduce_scatter(fx, fz, d_down)
    enc_cross_grad = lax.ppermute(oz[:, 1408:2688], "section", [(1, 0)])

    tokens_all = micro * lax.axis_size("dp") * length
    rates = tokens_all / (counts + tokens_all // 8)
    qkv_cols = jnp.arange(3 * width, dtype=jnp.int32) % width // HEAD_DIM >= HEADS // 2
    out_count = width // lax.axis_size("dp")
    out_rows = (lax.axis_index("dp") * out_count + jnp.arange(out_count, dtype=jnp.int32)) // HEAD_DIM >= HEADS // 2
    up_block = jnp.arange(hidden_width, dtype=jnp.int32) // FF_BLOCK
    up_rate = jnp.where(up_block == 0, rates[0], jnp.where(up_block == 1, rates[2], rates[3]))
    down_count = hidden_width // lax.axis_size("dp")
    down_block = (lax.axis_index("dp") * down_count + jnp.arange(down_count, dtype=jnp.int32)) // FF_BLOCK
    down_rate = jnp.where(down_block == 0, rates[0], jnp.where(down_block == 1, rates[2], rates[3]))
    layer_out = out.astype(bf16).reshape(stream.shape)
    stream_grad = d_in.astype(bf16).reshape(stream.shape)
    gain_grad = oz[:, 1280:1283].T[None]
    qkv_grad = (jnp.concatenate([ox[:, 3072:4352], oz[:, 640:1280]], axis=1) * jnp.where(qkv_cols, rates[1], rates[0])[None, :])[None]
    out_grad = (oz[:, :640] * jnp.where(out_rows, rates[1], rates[0])[:, None])[None]
    up_grad = (ox[:, :3072] * up_rate[None, :])[None]
    down_grad = (od * down_rate[:, None])[None]
    cross_grad = jnp.where(later, ox[:, 4352:5632], enc_cross_grad)[None]
    return (layer_out, stream_grad, gain_grad, qkv_grad, out_grad, up_grad, down_grad, cross_grad)


def solution(mesh):
    in_specs = (
        P("section", None, "dp", None, None),
        P("section", None, "dp", None, None),
        P(None, None, "dp"),
        P(None, "dp"),
        P(),
        P("section", None, None),
        P("section", None, None),
        P("section", None, None),
        P("section", None, None),
        P("section", None, None),
        P("section", None, None),
    )
    out_specs = (
        P("section", None, "dp", None, None),
        P("section", None, "dp", None, None),
        P("section", None, "dp"),
        P("section", "dp", None),
        P("section", "dp", None),
        P("section", "dp", None),
        P("section", "dp", None),
        P("section", "dp", None),
    )
    return jax.shard_map(shards, mesh=mesh, in_specs=in_specs, out_specs=out_specs, check_vma=False)
```

time: 1180 us -> 521 us (0.44)
  local copies, waits for them, and re-layouts: 318 us -> 48.5 us
  waiting for transfers between devices: 363 us -> 140 us
  matrix products: 279 us -> 102 us
  Pallas kernels: 0 us -> 70.7 us
  blocking collectives: 0 us -> 65.4 us
  other arithmetic: 107 us -> 62.5 us
  loops' own time: 53.6 us -> 9.79 us
  starting transfers between devices: 28.5 us -> 10.6 us
  between operations: 17.7 us -> 1.7 us
    reduce_scatter x1 -> x0, waiting for transfers between devices: 315 us -> none  [sum_packed(): lax.psum_scatter(lines, axis, tiled=True).reshape(-1)]
    ppermute x8 -> x6, waiting for transfers between devices: 38.6 us -> 140 us  [the longest x1 140 us: shards(): back = lax.ppermute(d_enc, 'section', [(1, 0)])]
    cond x261 -> x10, local copies, waits for them, and re-layouts: 82.7 us -> 2.65 us
    pallas_call x0 -> x1, Pallas kernels: none -> 70.7 us  [reduce_scatter(): pl.pallas_call(rs_kernel, out_shape=(jax.ShapeDtypeStruct((10, nx), f32),...]
    unnamed x93 -> x98, local copies, waits for them, and re-layouts: 75.8 us -> 7.51 us
    psum x0 -> x1, blocking collectives: none -> 65.4 us  [shards(): counts = lax.psum(counts, 'dp')]
    dot_general x28 -> x5, matrix products: 91.7 us -> 32.8 us  [project(): jnp.einsum('ayb,bc->ayc', barrier_operand, weight_matrix, preferred_eleme...]
    dot_general x16 -> x5, matrix products: 88 us -> 36.8 us  [weight_grad(): jnp.einsum('jxy,jxz->yz', barrier_operand, incoming_gradient, preferred_e...]
  transfers between devices with their start and end apart: 10 -> 6, of which waited for: 5 -> 1; matrix products, arithmetic and copies ran while one was open for 32% -> 6% of each run, Pallas kernels for 0% -> 0%
where the time goes in v1:
time: 521 us; the launch traced here: 511 us
  waiting for transfers between devices  140 us (27%)
  matrix products  102 us (20%)
  Pallas kernels  70.7 us (14%)
  blocking collectives  65.4 us (13%)
  other arithmetic  62.5 us (12%)
  local copies, waits for them, and re-layouts  48.5 us (9%)
  starting transfers between devices  10.6 us (2%)
  loops' own time  9.79 us (2%)
    ppermute x1, waiting for transfers between devices, shards(): back = lax.ppermute(d_enc, 'section', [(1, 0)])  140 us
    pallas_call x1, Pallas kernels, reduce_scatter(): pl.pallas_call(rs_kernel, out_shape=(jax.ShapeDtypeStruct((10, nx), f32),...  70.7 us
    psum x1, blocking collectives, shards(): counts = lax.psum(counts, 'dp')  65.4 us
    dot_general x5, matrix products, weight_grad(): jnp.einsum('jxy,jxz->yz', barrier_operand, incoming_gradient, preferred_e...  36.8 us
    dot_general x5, matrix products, project(): jnp.einsum('ayb,bc->ayc', barrier_operand, weight_matrix, preferred_eleme...  32.8 us
    dot_general x4, matrix products, project_back(): jnp.einsum('zhn,rn->zhr', incoming_gradient, weight_matrix, preferred_ele...  20.5 us
  transfers between devices with their start and end apart: 6, of which 1 were waited for; matrix products, arithmetic and copies ran while one was open for 6% of the time, Pallas kernels for 0%

profile of v1, /device:TPU:0, one launch (start us, length us, event | category | flops | bytes accessed | tf_op | source)
XLA Modules:
  0.0 511.1 jit_solution(990613123058452864)
XLA Ops:
  8.6 3.0 convolution_convert_fusion.2
  27.1 30.4 %conditional.3 = (f32[4,128,640]{2,1,0:T(8,128)}, bf16[4,128,640]{2,1,0:T(8,128)(2,1)}) conditional(s32[]{:T(128)} %convert_element_type.365, (f32[4,1,640]{2,0,1:T(4,128)S(1)}, f32[4,128,640]{2,1,0:T(8,128)}, f32[4,1,1]{0,2,1:T(1,128)S(1)}, f32[3,640]{1,0:T(4,128)S(1)}, bf16[640,3072]{1,0:T(8,128)(2,1)S(1)}, /*index=5*/f32[4,1,3072]{2,0,1:T(4,128)S(1)}, ...), branch_computations={%region_4.9_spmd, %region_9.10_spmd} | conditional | flops 4155442176 | bytes 31229008 | solution.py:543
  30.5 4.8 fusion.15
  35.3 17.7 %multiply_reduce_fusion.1 = (f32[4,128]{1,0:T(4,128)S(1)}, f32[4,128,640]{2,1,0:T(8,128)}) fusion(f32[4,640]{1,0:T(4,128)S(1)} %bitcast.358, f32[4,128,640]{2,1,0:T(8,128)} %get-tuple-element.375, f32[4,128]{1,0:T(4,128)S(1)} %bitcast.439, bf16[3072,640]{1,0:T(8,128)(2,1)S(1)} %get-tuple-element.381, f32[4,128,3072]{2,1,0:T(8,128)S(1)} %get-tuple-element.615, ...), kind=kOutput, calls=%fused_computation.32 | convolution fusion | flops 2123431424 | bytes 13301760 | tf_op jit(solution)/shard_map/cond/branch_0_fun/ayb,bc->ayc/dot_general | solution.py:280
  68.3 65.4 %psum.7 = s32[4]{0:T(128)S(1)} all-reduce(s32[4]{0:T(128)S(1)} %pad_add_fusion), channel_id=1, replica_groups=mesh['section'=2,'dp'=64] {'dp'}, use_global_device_ids=true, to_apply=%region_52.53 | all-reduce | flops 4 | bytes 32 | tf_op jit(solution)/shard_map/psum | solution.py:519
  141.1 2.8 copy.103
  146.4 20.4 %conditional.4 = (f32[4,128,640]{2,1,0:T(8,128)S(1)}, f32[4,128,640]{2,1,0:T(8,128)S(1)}, f32[640]{0:T(1024)S(1)}, f32[640]{0:T(1024)S(1)}, bf16[640,3072]{1,0:T...) conditional(s32[]{:T(128)} %convert_element_type.365, ...), branch_computations={%region_10.11_spmd, %region_11.27_spmd} | conditional | flops 22960414720 | bytes 400950688 | solution.py:565
  175.9 140.3 %collective-permute-done.4 = bf16[2,4,128,640]{3,2,1,0:T(8,128)(2,1)S(1)} collective-permute-done((bf16[2,4,128,640]{3,2,1,0:T(8,128)(2,1)}, bf16[2,4,128,640]{3,2,1,0:T(8,128)(2,1)S(1)}, u32[]{:S(2)}, u32[]{:S(2)}) %collective-permute-start.4) | collective-permute-done | bytes 1310752 | tf_op jit(solution)/shard_map/ppermute | solution.py:566
  316.3 56.4 %conditional.5 = (f32[4,128,640]{2,1,0:T(8,128)S(1)}, f32[4,128,640]{2,1,0:T(8,128)}, bf16[640,3072]{1,0:T(8,128)(2,1)}, f32[1,640]{1,0:T(1,128)S(1)}, f32[1,640...) conditional(s32[]{:T(128)} %convert_element_type.365, (f32[4,1,640]{2,0,1:T(4,128)S(1)}, ...), branch_computations={%region_27.43_spmd, %region_43.44_spmd} | conditional | flops 10661216256 | bytes 123853552 | solution.py:577
  320.0 3.0 fusion.224
  323.0 3.8 fusion.230
  326.9 5.2 %fusion.213 = (u8[128,3072]{1,0:T(8,128)(4,1)S(1)}, f32[4,128,3072]{2,1,0:T(8,128)S(1)}) fusion(bf16[640,3072]{1,0:T(8,128)(2,1)S(1)} %copy-done.94, f32[640]{0:T(1024)S(1)} %get-tuple-element.601, f32[4,128]{1,0:T(4,128)S(1)} %add_rsqrt_fusion.6, f32[4,640]{1,0:T(4,128)S(1)} %bitcast.383, f32[4,128,640]{2,1,0:T(8,128)} %get-tuple-element.420, ...), kind=kOutput, calls=%fused_computation.286 | convolution fusion | flops 2027094016 | bytes 11944448 | tf_op jit(solution)/shard_map/cond/branch_0_fun/ayb,bc->ayc/dot_general | solution.py:280
  332.2 17.6 %bitcast_convert_fusion.4 = bf16[3072,640]{1,0:T(8,128)(2,1)} fusion(f32[4,128,3072]{2,1,0:T(8,128)S(1)} %get-tuple-element.662, f32[4,3072]{1,0:T(4,128)S(1)} %bitcast.415, u8[128,3072]{1,0:T(8,128)(4,1)S(1)} %get-tuple-element.661, f32[4,128,640]{2,1,0:T(8,128)S(1)} %get-tuple-element.647, f32[4,128]{1,0:T(4,128)S(1)} %bitcast.446, ...), kind=kOutput, calls=%fused_computation.247 | convolution fusion | flops 2124742656 | bytes 11988992 | tf_op jit(solution)/shard_map/cond/branch_0_fun/jxy,jxz->yz/dot_general | solution.py:292
  349.8 6.9 %fusion.193 = bf16[4,128,3072]{2,1,0:T(8,128)(2,1)} fusion(f32[4,128,3072]{2,1,0:T(8,128)S(1)} %get-tuple-element.662, bf16[3072,640]{1,0:T(8,128)(2,1)S(1)} %copy-done.98, f32[4,3072]{1,0:T(4,128)S(1)} %bitcast.416, f32[4,128,640]{2,1,0:T(8,128)S(1)} %get-tuple-element.647, f32[4,128]{1,0:T(4,128)S(1)} %bitcast.447, f32[4,640]{1,0:T(4,128)S(1)} %bitcast.385), kind=kOutput, calls=%fused_computation.254 | convolution fusion | flops 2031550464 | bytes 14741504 | tf_op jit(solution)/shard_map/cond/branch_0_fun/zhn,rn->zhr/dot_general | solution.py:286
  356.7 7.3 %bitcast_convert_fusion.5 = bf16[640,3072]{1,0:T(8,128)(2,1)} fusion(bf16[4,128,3072]{2,1,0:T(8,128)(2,1)} %fusion.193, s32[640]{0:T(1024)S(1)} %get-tuple-element.426, f32[640]{0:T(1024)S(1)} %get-tuple-element.601, f32[4,128]{1,0:T(4,128)S(1)} %add_rsqrt_fusion.6, f32[4,640]{1,0:T(4,128)S(1)} %bitcast.386, f32[4,128,640]{2,1,0:T(8,128)} %get-tuple-element.420, ...), kind=kOutput, calls=%fused_computation.248 | convolution fusion | flops 2437038080 | bytes 8408064 | tf_op jit(solution)/shard_map/cond/branch_0_fun/jxy,jxz->yz/dot_general | solution.py:292
  364.0 6.4 %multiply_reduce_fusion.13 = (f32[640]{0:T(1024)S(1)}, f32[4,128]{1,0:T(4,128)S(1)}, f32[4,128]{1,0:T(4,128)S(1)}, f32[4,128,640]{2,1,0:T(8,128)S(1)}) fusion(f32[4,128]{1,0:T(4,128)S(1)} %add_rsqrt_fusion.6, f32[4,640]{1,0:T(4,128)S(1)} %bitcast.387, f32[4,128,640]{2,1,0:T(8,128)} %get-tuple-element.420, f32[4,128]{1,0:T(4,128)S(1)} %get-tuple-element.652, ...), kind=kOutput, calls=%fused_computation.303 | convolution fusion | flops 2016541056 | bytes 9722880 | tf_op jit(solution)/shard_map/cond/branch_0_fun/zhn,rn->zhr/dot_general | solution.py:286
  394.0 4.4 fusion.276
  398.5 4.4 multiply_reduce_fusion.22
  402.9 3.6 bitcast_convert_fusion.6
  407.2 4.0 bitcast_convert_fusion.7
  415.9 6.5 %pad_maximum_fusion.9 = bf16[640,5632]{1,0:T(8,128)(2,1)} fusion(bf16[640,1280]{1,0:T(8,128)(2,1)} %get-tuple-element.572, bf16[640,1280]{1,0:T(8,128)(2,1)} %fusion.276, bf16[640,3072]{1,0:T(8,128)(2,1)} %get-tuple-element.471), kind=kLoop, calls=%fused_computation.371 | loop fusion | flops 21626880 | bytes 14417920 | tf_op jit(solution)/shard_map/concatenate | solution.py:586
  422.4 3.1 fusion.275
  425.5 70.7 %sum_gradients.1 = (f32[10,5632]{1,0:T(8,128)}, f32[10,2688]{1,0:T(8,128)}, f32[48,640]{1,0:T(8,128)}) custom-call(bf16[2,4,80,5632]{3,2,1,0:T(8,128)(2,1)} %bitcast.342, bf16[2,4,80,2688]{3,2,1,0:T(8,128)(2,1)} %bitcast.344, bf16[4,2,4,2,48,640]{5,4,3,2,1,0:T(8,128)(2,1)} %get-tuple-element.476.dn), custom_call_target="tpu_custom_call" | custom-call | tf_op jit(solution)/shard_map/sum_gradients/pallas_call | solution.py:267
  501.9 3.6 fusion.343
  (225 shorter events, 115.1 us)
Async XLA Ops:
  2.9 133.9 %copy-start.71 = (s32[4]{0:T(128)}, s32[4]{0:T(128)S(1)}, u32[]{:S(2)}) copy-start(s32[4]{0:T(128)S(1)} %get-tuple-element.607) | copy-start | bytes 52
  4.6 141.7 %copy-start.73 = (f32[4,128,1]{1,0,2:T(4,128)}, f32[4,128,1]{1,0,2:T(4,128)S(1)}, u32[]{:S(2)}) copy-start(f32[4,128,1]{1,0,2:T(4,128)S(1)} %fusion.403) | copy-start | bytes 6148
  4.8 141.6 %copy-start.33 = (f32[4,1,3072]{2,0,1:T(4,128)}, f32[4,1,3072]{2,0,1:T(4,128)S(1)}, u32[]{:S(2)}) copy-start(f32[4,1,3072]{2,0,1:T(4,128)S(1)} %fusion.345) | copy-start | bytes 147460
  8.5 137.8 %copy-start.41 = (f32[3,640]{1,0:T(4,128)}, f32[3,640]{1,0:T(4,128)S(1)}, u32[]{:S(2)}) copy-start(f32[3,640]{1,0:T(4,128)S(1)} %get-tuple-element.670) | copy-start | bytes 23044
  27.1 37.1 %copy-start.72 = (bf16[1,3,640]{2,1,0:T(4,128)(2,1)S(1)}, bf16[1,3,640]{2,1,0:T(4,128)(2,1)}, u32[]{:S(2)}) copy-start(bf16[1,3,640]{2,1,0:T(4,128)(2,1)} %param.22) | copy-start | bytes 11524
  27.1 109.1 %copy-start.91 = (s32[2,4,1]{1,2,0:T(1,128)S(1)}, s32[2,4,1]{1,2,0:T(1,128)}, u32[]{:S(2)}) copy-start(s32[2,4,1]{1,2,0:T(1,128)} %param.19) | copy-start | bytes 100
  57.5 86.4 %collective-permute-start = (bf16[4,128,640]{2,1,0:T(8,128)(2,1)}, bf16[4,128,640]{2,1,0:T(8,128)(2,1)}, u32[]{:S(2)}, u32[]{:S(2)}) collective-permute-start(bf16[4,128,640]{2,1,0:T(8,128)(2,1)} %get-tuple-element.461), channel_id=1, source_target_pairs={{0,64},{1,65},{2,66},{3,67},{4,68},{5,69},{6,70},{7,71},{8,72},{9,... | collective-permute-start | bytes 1966088 | tf_op jit(solution)/shard_map/ppermute | solution.py:544
  59.7 84.3 %collective-permute-start.3 = (bf16[640,1280]{1,0:T(8,128)(2,1)}, bf16[640,1280]{1,0:T(8,128)(2,1)}, u32[]{:S(2)}, u32[]{:S(2)}) collective-permute-start(bf16[640,1280]{1,0:T(8,128)(2,1)} %bitcast.410), channel_id=1, source_target_pairs={{0,64},{1,65},{2,66},{3,67},{4,68},{5,69},{6,70},{7,71},{8,72},{9,... | collective-permute-start | bytes 4915208 | tf_op jit(solution)/shard_map/ppermute | solution.py:511
  62.1 81.8 %collective-permute-start.1 = (bf16[4,128,640]{2,1,0:T(8,128)(2,1)S(1)}, bf16[4,128,640]{2,1,0:T(8,128)(2,1)}, u32[]{:S(2)}, u32[]{:S(2)}) collective-permute-start(bf16[4,128,640]{2,1,0:T(8,128)(2,1)S(1)} %bitcast.343), channel_id=1, source_target_pairs={{0,64},{1,65},{2,66},{3,67},{4,68},{5,69},{6,70},{7,71},{8,72},{9,... | collective-permute-start | bytes 1966088 | tf_op jit(solution)/shard_map/ppermute | solution.py:509
  64.3 79.7 %collective-permute-start.2 = (bf16[1,640]{1,0:T(2,128)(2,1)S(1)}, bf16[1,640]{1,0:T(2,128)(2,1)S(1)}, u32[]{:S(2)}, u32[]{:S(2)}) collective-permute-start(bf16[1,640]{1,0:T(2,128)(2,1)S(1)} %slice_bitcast_fusion.4), channel_id=1, source_target_pairs={{0,64},{1,65},{2,66},{3,67},{4,68},{5,69},{6,70},{7,71},{8,72},{9,... | collective-permute-start | bytes 3848 | tf_op jit(solution)/shard_map/ppermute | solution.py:510
  68.3 75.6 %copy-start.43 = (s32[640]{0:T(1024)}, s32[640]{0:T(1024)S(1)}, u32[]{:S(2)}) copy-start(s32[640]{0:T(1024)S(1)} %add_select_fusion.18) | copy-start | bytes 7684
  166.8 149.4 %collective-permute-start.4 = (bf16[2,4,128,640]{3,2,1,0:T(8,128)(2,1)}, bf16[2,4,128,640]{3,2,1,0:T(8,128)(2,1)S(1)}, u32[]{:S(2)}, u32[]{:S(2)}) collective-permute-start(bf16[2,4,128,640]{3,2,1,0:T(8,128)(2,1)} %get-tuple-element.463), channel_id=1, source_target_pairs={{64,0},{65,1},{66,2},{67,3},{68,4},{69,5},{70,6},{71,7},{72,8},{73... | collective-permute-start | bytes 3932168 | tf_op jit(solution)/shard_map/ppermute | solution.py:566
  174.8 141.4 %copy-start.6 = (f32[4,128,640]{2,1,0:T(8,128)S(1)}, f32[4,128,640]{2,1,0:T(8,128)}, u32[]{:S(2)}) copy-start(f32[4,128,640]{2,1,0:T(8,128)} %bitcast_convert_fusion.8) | copy-start | bytes 3932164
  174.8 141.4 %copy-start.34 = (f32[4,1,3072]{2,0,1:T(4,128)S(1)}, f32[4,1,3072]{2,0,1:T(4,128)}, u32[]{:S(2)}) copy-start(f32[4,1,3072]{2,0,1:T(4,128)} %copy-done.33) | copy-start | bytes 147460
  174.8 141.3 %copy-start.42 = (f32[3,640]{1,0:T(4,128)S(1)}, f32[3,640]{1,0:T(4,128)}, u32[]{:S(2)}) copy-start(f32[3,640]{1,0:T(4,128)} %copy-done.41) | copy-start | bytes 23044
  174.9 141.3 %copy-start.61 = (f32[640]{0:T(1024)S(1)}, f32[640]{0:T(1024)}, u32[]{:S(2)}) copy-start(f32[640]{0:T(1024)} %copy-done.60) | copy-start | bytes 7684
  174.9 141.3 %copy-start.64 = (f32[640]{0:T(1024)S(1)}, f32[640]{0:T(1024)}, u32[]{:S(2)}) copy-start(f32[640]{0:T(1024)} %copy-done.63) | copy-start | bytes 7684
  174.9 141.3 %copy-start.74 = (f32[4,128,1]{1,0,2:T(4,128)S(1)}, f32[4,128,1]{1,0,2:T(4,128)}, u32[]{:S(2)}) copy-start(f32[4,128,1]{1,0,2:T(4,128)} %copy-done.73) | copy-start | bytes 6148
  174.9 141.3 %copy-start.89 = (s32[640]{0:T(1024)S(1)}, s32[640]{0:T(1024)}, u32[]{:S(2)}) copy-start(s32[640]{0:T(1024)} %get-tuple-element.688) | copy-start | bytes 7684
  316.2 57.5 %copy-start.32 = (f32[4,640]{1,0:T(4,128)S(1)}, f32[4,640]{1,0:T(4,128)}, u32[]{:S(2)}) copy-start(f32[4,640]{1,0:T(4,128)} %copy-done.31) | copy-start | bytes 30724
  316.2 57.5 %copy-start.85 = (f32[4,128]{1,0:T(4,128)S(1)}, f32[4,128]{1,0:T(4,128)}, u32[]{:S(2)}) copy-start(f32[4,128]{1,0:T(4,128)} %copy-done.84) | copy-start | bytes 6148
  425.5 72.9 %copy-start.90 = (f32[10]{0:T(128)S(1)}, f32[10]{0:T(128)}, u32[]{:S(2)}) copy-start(f32[10]{0:T(128)} %compare_select_fusion.3) | copy-start | bytes 124
  425.5 76.3 %copy-start.87 = (f32[4]{0:T(128)S(1)}, f32[4]{0:T(128)}, u32[]{:S(2)}) copy-start(f32[4]{0:T(128)} %copy-done.86) | copy-start | bytes 52
  497.1 11.2 %collective-permute-start.5 = (f32[10,1280]{1,0:T(8,128)S(1)}, f32[10,1280]{1,0:T(8,128)S(1)}, u32[]{:S(2)}, u32[]{:S(2)}) collective-permute-start(f32[10,1280]{1,0:T(8,128)S(1)} %slice.185), channel_id=1, source_target_pairs={{64,0},{65,1},{66,2},{67,3},{68,4},{69,5},{70,6},{71,7},{72,8},{73... | collective-permute-start | bytes 153608 | tf_op jit(solution)/shard_map/ppermute | solution.py:589
  (32 other events, 198.0 us)

commit v2 on v0

v2 whole, which is shorter than its diff:
```python
import functools

import jax
import jax.numpy as jnp
from jax import lax
from jax.experimental import pallas as pl
from jax.experimental.pallas import tpu as pltpu
from jax.sharding import PartitionSpec as P

F32, BF16 = jnp.float32, jnp.bfloat16
D, HEADS, HEAD_DIM, FF, FF_BLOCK = 640, 8, 80, 3072, 1024
SEQ, SENTENCES = 128, 4
ROWS = SEQ * SENTENCES
HALF = ROWS // 2
TILE = 512
EPSILON = 1e-05
NEGATIVE = -1e30
SCALE = HEAD_DIM ** (-0.5)
LOG2E = 1.4426950408889634
MESH = pl.DeviceIdType.MESH
VMEM_LIMIT = 62 * 1024 * 1024
NX, NY, NZ, CORES = 4, 2, 4, 2


def place():
    me = lax.axis_index("dp")
    core = me % CORES
    z = me // CORES % NZ
    y = me // (CORES * NZ) % NY
    x = me // (CORES * NZ * NY)
    return x, y, z, core


def device_at(x, y, z, core):
    return {"dp": ((x * NY + y) * NZ + z) * CORES + core}


def relative_order(first):
    x, y, z, core = place()
    spot = jnp.arange(D, dtype=jnp.int32)
    rc, ra, rb, ry, t = spot // 320, spot // 80 % 4, spot // 20 % 4, spot // 10 % 2, spot % 10
    rx, rz = (ra, rb) if first == "x" else (rb, ra)
    cx, cy, cz, cc = (x + rx) % 4, (y + ry) % 2, (z + rz) % 4, (core + rc) % 2
    return (((cx * 2 + cy) * 4 + cz) * 2 + cc) * 10 + t


def mm(a, b):
    return lax.dot_general(a, b, (((1,), (0,)), ((), ())), preferred_element_type=F32)


def mm_nt(a, b):
    return lax.dot_general(a, b, (((1,), (1,)), ((), ())), preferred_element_type=F32)


def mm_tn(a, b):
    return lax.dot_general(a, b, (((0,), (0,)), ((), ())), preferred_element_type=F32)


def block(m, size=SEQ):
    if isinstance(m, int):
        return pl.ds(m * size, size)
    return pl.ds(pl.multiple_of(m * size, size), size)


def each(lo, count, body):
    def step(i, _):
        body(lo + i)
        return 0

    lax.fori_loop(0, count, step, 0)


def normalize(v, mask, inv_width):
    centred = (v - jnp.sum(v * mask, -1, keepdims=True) * inv_width) * mask
    spread = jnp.sum(centred * centred, -1, keepdims=True) * inv_width
    inverse = lax.rsqrt(spread + EPSILON)
    return centred * inverse, inverse


def normalize_back(dn, normed, inverse, mask, inv_width):
    dn = dn * mask
    first = jnp.sum(dn, -1, keepdims=True) * inv_width
    second = jnp.sum(dn * normed, -1, keepdims=True) * inv_width
    return inverse * (dn - (first + normed * second) * mask)


def window(h):
    return HEAD_DIM * h // 128 * 128, -(-HEAD_DIM * (h + 1) // 128) * 128


def head_lanes(h):
    lo, hi = window(h)
    lanes = lax.broadcasted_iota(jnp.int32, (1, hi - lo), 1) + lo
    return ((lanes >= HEAD_DIM * h) & (lanes < HEAD_DIM * (h + 1))).astype(F32).astype(BF16)


class Tiles:
    def __init__(self):
        self.tile = {}

    def add(self, h, value):
        lo, hi = window(h)
        for j in range(lo // 128, hi // 128):
            part = value[:, j * 128 - lo : j * 128 - lo + 128]
            self.tile[j] = self.tile[j] + part if j in self.tile else part

    def whole(self):
        return jnp.concatenate([self.tile[j] for j in range(D // 128)], axis=1)


class Sentence:
    def __init__(self, meta, m):
        self.meta, self.m = meta, m
        lanes = lax.broadcasted_iota(jnp.int32, (1, D), 1)
        self.mask = (lanes < meta[m, 0]).astype(F32)
        self.heads = (lanes < meta[m, 1]).astype(F32)
        self.inv = 1.0 / meta[m, 0].astype(F32)

    def rows(self):
        return (lax.broadcasted_iota(jnp.int32, (SEQ, 1), 0) < self.meta[self.m, 4]).astype(F32)

    def self_bias(self):
        k = lax.broadcasted_iota(jnp.int32, (SEQ, SEQ), 0)
        q = lax.broadcasted_iota(jnp.int32, (SEQ, SEQ), 1)
        allowed = (k < self.meta[self.m, 4]) & (k <= q + (1 - self.meta[self.m, 6]) * SEQ)
        return jnp.where(allowed, 0.0, NEGATIVE)

    def cross_bias(self):
        k = lax.broadcasted_iota(jnp.int32, (2 * SEQ, 1), 0)
        allowed = (jnp.where(k < SEQ, k, k - SEQ) < self.meta[self.m, 5]) & (k < self.meta[self.m, 3])
        return jnp.where(allowed, 0.0, NEGATIVE)


def softmax_columns(scores, bias):
    scores = scores + bias
    exponent = jnp.exp2((scores - jnp.max(scores, 0, keepdims=True)) * (SCALE * LOG2E))
    return (exponent * (1.0 / jnp.sum(exponent, 0, keepdims=True))).astype(BF16)


def attend(query, keys, values, bias, keep):
    scores = [mm_nt(keys(h), query(h) * head_lanes(h)) for h in range(HEADS)]
    weights = [softmax_columns(s, bias) for s in scores]
    out = Tiles()
    for h in range(HEADS):
        keep(h, weights[h])
        out.add(h, mm_tn(weights[h], values(h) * head_lanes(h)))
    return out.whole()


def attend_back(d_out, query, keys, values, weights):
    d_weights = [mm_nt(values(h), d_out(h) * head_lanes(h)) for h in range(HEADS)]
    d_values = Tiles()
    for h in range(HEADS):
        d_values.add(h, mm(weights(h), d_out(h) * head_lanes(h)))
    d_values = d_values.whole().astype(BF16)
    d_scores = []
    for h in range(HEADS):
        p = weights(h).astype(F32)
        product = p * d_weights[h]
        d_scores.append((product - p * jnp.sum(product, 0, keepdims=True)).astype(BF16))
    d_keys = Tiles()
    for h in range(HEADS):
        d_keys.add(h, mm(d_scores[h], query(h) * head_lanes(h)))
    d_keys = (d_keys.whole() * SCALE).astype(BF16)
    d_query = Tiles()
    for h in range(HEADS):
        d_query.add(h, mm_tn(d_scores[h], keys(h) * head_lanes(h)))
    return (d_query.whole() * SCALE).astype(BF16), d_keys, d_values


def gelu_pair(z):
    cdf = 0.5 + 0.5 * lax.erf(z * 0.7071067811865476)
    density = jnp.exp2(z * z * (-0.5 * LOG2E)) * 0.3989422804014327
    return z * cdf, cdf + z * density


def shape(*dims, dtype=BF16):
    return jax.ShapeDtypeStruct(dims, dtype)


IN_VMEM = pl.BlockSpec(memory_space=pltpu.VMEM)
IN_SMEM = pl.BlockSpec(memory_space=pltpu.SMEM)
IN_HBM = pl.BlockSpec(memory_space=pl.ANY)


def layers_kernel(meta, x_hbm, cot_hbm, gain_ref, wqkv_hbm, wout_hbm, wup_hbm, wdn_hbm, wcross_hbm, picks_hbm,
                  out_hbm, dx_hbm, extra_hbm, a_hbm, qkv_hbm, o_hbm, p_hbm, gsum_ref, dup_hbm, ddn_hbm, dcross_hbm, dwc_hbm,
                  x, cot, xenc, genc, wqkv, wout, wup, wdn, wcross, wc, picks,
                  a, qkv, o, p, x1, c, qc, ebuf, sbuf, kv, oc, pc, mid, b, u, g, lo, dbr, dbrc, dx, tmp, stage_up, stage_dn,
                  load_sem, out_sem, send_sem, recv_sem):
    section = lax.axis_index("section")
    px, py, pz, core = place()
    partner = {"section": 1 - section, "dp": lax.axis_index("dp")}
    across = {"section": 1 - section, **device_at(px, 1 - py, pz, core)}
    sibling = {"section": section, **device_at(px, py, pz, 1 - core)}
    barrier = pltpu.get_barrier_semaphore()
    for d in (partner, across, sibling):
        pl.semaphore_signal(barrier, inc=1, device_id=d, device_id_type=MESH)

    def load(k, src, dst):
        return pltpu.make_async_copy(src, dst, load_sem.at[k])

    def store(k, src, dst):
        return pltpu.make_async_copy(src, dst, out_sem.at[k])

    def remote(k, src, dst, device):
        return pltpu.make_async_remote_copy(
            src_ref=src, dst_ref=dst, send_sem=send_sem.at[k], recv_sem=recv_sem.at[k], device_id=device, device_id_type=MESH)

    get_x, get_qkv, get_out = load(0, x_hbm, x), load(1, wqkv_hbm, wqkv), load(2, wout_hbm, wout)
    get_up, get_dn, get_cross = load(3, wup_hbm, wup), load(4, wdn_hbm, wdn), load(5, wcross_hbm, wcross)
    get_cot, get_picks = load(6, cot_hbm, cot), load(7, picks_hbm, picks)
    for k in (get_x, get_qkv, get_out, get_up, get_dn, get_cross, get_cot, get_picks):
        k.start()
    pl.semaphore_wait(barrier, 3)
    part = pl.ds(pl.multiple_of(core * 320, 320), 320)
    rest = pl.ds(pl.multiple_of((1 - core) * 320, 320), 320)
    send_x = remote(0, x_hbm, xenc, partner)
    send_gain = remote(1, gain_ref, genc, partner)
    send_wc = remote(2, wcross_hbm.at[part], wc.at[part], across)
    share_wc = remote(3, wc.at[part], wc.at[part], sibling)

    def send_new(m):
        return remote(4 + m, sbuf.at[m, pl.ds(0, SEQ)], ebuf.at[m, pl.ds(0, SEQ)], partner)

    def send_old(m):
        return remote(8 + m, sbuf.at[m, pl.ds(SEQ, SEQ)], ebuf.at[m, pl.ds(SEQ, SEQ)], partner)

    @pl.when(section == 0)
    def _():
        send_gain.start()
        send_wc.start()
        send_x.start()

    gsum_ref[...] = jnp.zeros_like(gsum_ref)
    gain = [gain_ref[i : i + 1] for i in range(3)]

    get_x.wait()

    def norm_x(m):
        s = Sentence(meta, m)
        a[block(m)] = (normalize(x[block(m)].astype(F32), s.mask, s.inv)[0] * gain[0]).astype(BF16)

    each(0, SENTENCES, norm_x)
    get_qkv.wait()

    def project(j):
        qkv[:, block(j, D)] = mm(a[...], wqkv[:, block(j, D)]).astype(BF16)

    each(0, 3, project)
    keep = [store(0, a, a_hbm), store(1, qkv, qkv_hbm)]
    for k in keep:
        k.start()

    def self_attention(m):
        s = Sentence(meta, m)
        rows = block(m)

        def keep_p(h, value):
            p[m * HEADS + h] = value

        blended = attend(
            lambda h: qkv[rows, slice(*window(h))],
            lambda h: qkv[rows, D + window(h)[0] : D + window(h)[1]],
            lambda h: qkv[rows, 2 * D + window(h)[0] : 2 * D + window(h)[1]],
            s.self_bias(), keep_p)
        o[rows] = (blended * s.heads).astype(BF16)

    each(0, SENTENCES, self_attention)
    keep += [store(2, o, o_hbm), store(3, p, p_hbm)]
    for k in keep[2:]:
        k.start()
    get_out.wait()
    x1[...] = mm(o[...], wout[...])

    def add_attention(m):
        s = Sentence(meta, m)
        rows = block(m)
        x1[rows] = x[rows].astype(F32) + x1[rows] * s.mask * s.rows()

    each(0, SENTENCES, add_attention)

    def ffn_forward(half, base, g_row, finish):
        rows = block(half, HALF)

        def norm(m):
            s = Sentence(meta, m)
            b[block(m)] = (normalize(base[block(m)], s.mask, s.inv)[0] * gain[g_row]).astype(BF16)

        each(2 * half, 2, norm)
        live = [[(t * TILE < meta[2 * half + i, 2]).astype(F32) for t in range(FF // TILE)] for i in range(2)]
        z = mm(b[rows], wup[:, 0:TILE])
        for t in range(FF // TILE):
            after = mm(b[rows], wup[:, (t + 1) * TILE : (t + 2) * TILE]) if t + 1 < FF // TILE else None
            cols = pl.ds(t * TILE, TILE)
            for i in range(2):
                value, slope = gelu_pair(z[i * SEQ : (i + 1) * SEQ])
                u[block(2 * half + i), cols] = (value * live[i][t]).astype(BF16)
                g[block(2 * half + i), cols] = (slope * live[i][t]).astype(BF16)
            z = after
        tmp[...] = mm(u[rows], wdn[...])

        def result(i):
            m = 2 * half + i
            s = Sentence(meta, m)
            value = base[block(m)] + tmp[block(i)] * s.mask * s.rows()
            lo[block(m)] = value.astype(BF16)
            finish(m, s, value)

        each(0, 2, result)

    def ffn_back(half, base, g_row):
        rows = block(half, HALF)
        for t in range(FF // TILE):
            cols = pl.ds(t * TILE, TILE)
            g[rows, cols] = (mm_nt(dbr[rows], wdn[cols]) * g[rows, cols].astype(F32)).astype(BF16)
        tmp[...] = mm_nt(g[rows], wup[...])

        def result(i):
            m = 2 * half + i
            s = Sentence(meta, m)
            n, r = normalize(base[block(m)], s.mask, s.inv)
            dy = tmp[block(i)]
            gsum_ref[g_row : g_row + 1] += jnp.sum(dy * n, 0, keepdims=True)
            dx[block(m)] += normalize_back(dy * gain[g_row], n, r, s.mask, s.inv)

        each(0, 2, result)

    def turned(k, value):
        return mm_nt(picks[k], value).astype(BF16)

    def ffn_weights():
        bt = turned(0, b[...])
        pieces = []
        for t in range(FF // FF_BLOCK):
            slot = t % 2
            cols = pl.ds(t * FF_BLOCK, FF_BLOCK)
            if t >= 2:
                for k in pieces[2 * (t - 2) : 2 * (t - 1)]:
                    k.wait()
            stage_dn[slot] = mm_tn(u[:, cols], dbr[...]).astype(BF16)
            stage_up[slot] = mm(bt, g[:, cols]).astype(BF16)
            pieces += [store(4 + 2 * t, stage_dn.at[slot], ddn_hbm.at[cols]), store(5 + 2 * t, stage_up.at[slot], dup_hbm.at[:, cols])]
            for k in pieces[-2:]:
                k.start()
        return pieces[2:]

    @pl.when(section == 0)
    def _():
        get_up.wait()
        get_dn.wait()

        def forward(half):
            def finish(m, s, value):
                mid[block(m)] = value
                sbuf[m, 0:SEQ] = (normalize(value, s.mask, s.inv)[0] * gain[2]).astype(BF16)
                send_new(m).start()

            ffn_forward(half, x1, 1, finish)

        each(0, 2, forward)
        put_out = store(10, lo, out_hbm)
        put_out.start()
        get_cot.wait()

        def backward(half):
            def start(i):
                m = 2 * half + i
                s = Sentence(meta, m)
                send_new(m).wait_recv()
                n, r = normalize(mid[block(m)], s.mask, s.inv)
                dy = ebuf[m, 0:SEQ].astype(F32)
                gsum_ref[2:3] += jnp.sum(dy * n, 0, keepdims=True)
                d = cot[block(m)].astype(F32) + normalize_back(dy * gain[2], n, r, s.mask, s.inv)
                dx[block(m)] = d
                dbr[block(m)] = (d * s.mask * s.rows()).astype(BF16)

            each(0, 2, start)
            ffn_back(half, x1, 1)

        each(0, 2, backward)
        get_picks.wait()
        put_dx = store(11, dx, dx_hbm)
        put_dx.start()
        pieces = ffn_weights()

        def old(m):
            s = Sentence(meta, m)
            send_old(m).wait_recv()
            n, r = normalize(x[block(m)].astype(F32), s.mask, s.inv)
            dy = ebuf[m, SEQ : 2 * SEQ].astype(F32)
            gsum_ref[2:3] += jnp.sum(dy * n, 0, keepdims=True)
            mid[block(m)] = normalize_back(dy * gain[2], n, r, s.mask, s.inv)

        each(0, SENTENCES, old)
        put_extra = store(12, mid, extra_hbm)
        put_extra.start()
        get_cross.wait()
        for k in (put_out, put_dx, put_extra, *pieces):
            k.wait()
        send_x.wait_send()
        send_gain.wait_send()
        send_wc.wait_send()
        each(0, SENTENCES, lambda m: send_new(m).wait_send())

    @pl.when(section == 1)
    def _():
        get_cross.wait()

        def norm(m):
            s = Sentence(meta, m)
            c[block(m)] = (normalize(x1[block(m)], s.mask, s.inv)[0] * gain[1]).astype(BF16)

        each(0, SENTENCES, norm)
        qc[...] = mm(c[...], wcross[:, 0:D]).astype(BF16)
        send_gain.wait_recv()
        send_x.wait_recv()

        def old(m):
            s = Sentence(meta, m)
            ebuf[m, SEQ : 2 * SEQ] = (normalize(xenc[block(m)].astype(F32), s.mask, s.inv)[0] * genc[2:3]).astype(BF16)

        each(0, SENTENCES, old)
        send_wc.wait_recv()
        share_wc.start()
        share_wc.wait_recv()

        def old_kv(m):
            kv[m, SEQ : 2 * SEQ] = mm(ebuf[m, SEQ : 2 * SEQ], wc[...]).astype(BF16)

        each(0, SENTENCES, old_kv)
        get_cot.wait()
        get_up.wait()
        get_dn.wait()

        def start_back(m):
            s = Sentence(meta, m)
            d = cot[block(m)].astype(F32)
            dx[block(m)] = d
            dbr[block(m)] = (d * s.mask * s.rows()).astype(BF16)

        each(0, SENTENCES, start_back)

        def middle(half):
            rows = block(half, HALF)

            def new_kv(m):
                send_new(m).wait_recv()
                kv[m, 0:SEQ] = mm(ebuf[m, 0:SEQ], wc[...]).astype(BF16)

            each(2 * half, 2, new_kv)

            def cross(m):
                s = Sentence(meta, m)

                def keep_p(h, value):
                    pc[m * HEADS + h] = value

                blended = attend(
                    lambda h: qc[block(m), slice(*window(h))],
                    lambda h: kv[m, :, slice(*window(h))],
                    lambda h: kv[m, :, D + window(h)[0] : D + window(h)[1]],
                    s.cross_bias(), keep_p)
                oc[block(m)] = (blended * s.heads).astype(BF16)

            each(2 * half, 2, cross)
            tmp[...] = mm(oc[rows], wcross[:, D : 2 * D])

            def add_cross(i):
                m = 2 * half + i
                s = Sentence(meta, m)
                mid[block(m)] = x1[block(m)] + tmp[block(i)] * s.mask * s.rows()

            each(0, 2, add_cross)
            ffn_forward(half, mid, 2, lambda m, s, value: None)
            ffn_back(half, mid, 2)

            def branch(m):
                s = Sentence(meta, m)
                dbrc[block(m)] = (dx[block(m)] * s.mask * s.rows()).astype(BF16)

            each(2 * half, 2, branch)
            tmp[...] = mm_nt(dbrc[rows], wcross[:, D : 2 * D])

            def cross_back(i):
                m = 2 * half + i
                s = Sentence(meta, m)
                sbuf[m, 0:SEQ] = (tmp[block(i)] * s.heads).astype(BF16)
                dq, dk, dv = attend_back(
                    lambda h: sbuf[m, 0:SEQ, slice(*window(h))],
                    lambda h: qc[block(m), slice(*window(h))],
                    lambda h: kv[m, :, slice(*window(h))],
                    lambda h: kv[m, :, D + window(h)[0] : D + window(h)[1]],
                    lambda h: pc[m * HEADS + h])
                qc[block(m)] = dq
                kv[m, :, 0:D] = dk
                kv[m, :, D : 2 * D] = dv
                sbuf[m] = mm_nt(kv[m], wc[...]).astype(BF16)
                send_new(m).start()

            each(0, 2, cross_back)
            each(2 * half, 2, lambda m: send_old(m).start())
            tmp[...] = mm_nt(qc[rows], wcross[:, 0:D])

            def first_norm(i):
                m = 2 * half + i
                s = Sentence(meta, m)
                n, r = normalize(x1[block(m)], s.mask, s.inv)
                dy = tmp[block(i)]
                gsum_ref[1:2] += jnp.sum(dy * n, 0, keepdims=True)
                dx[block(m)] += normalize_back(dy * gain[1], n, r, s.mask, s.inv)

            each(0, 2, first_norm)

        each(0, 2, middle)
        put_out = store(10, lo, out_hbm)
        put_out.start()
        put_dx = store(11, dx, dx_hbm)
        put_dx.start()
        get_picks.wait()
        pieces = ffn_weights()
        for k in pieces:
            k.wait()
        stage_up[0, :, 0:D] = mm(turned(0, c[...]), qc[...]).astype(BF16)
        put_q = store(13, stage_up.at[0, :, pl.ds(0, D)], dcross_hbm.at[:, pl.ds(0, D)])
        put_q.start()
        stage_up[1, :, 0:D] = mm(turned(0, oc[...]), dbrc[...]).astype(BF16)
        put_o = store(14, stage_up.at[1, :, pl.ds(0, D)], dcross_hbm.at[:, pl.ds(D, D)])
        put_o.start()
        et = turned(1, ebuf[...].reshape(2 * ROWS, D))
        wcross[...] = mm(et, kv[...].reshape(2 * ROWS, 2 * D)).astype(BF16)
        put_wc = store(12, wcross, dwc_hbm)
        put_wc.start()
        for k in (put_out, put_dx, put_q, put_o, put_wc):
            k.wait()
        share_wc.wait_send()
        each(0, SENTENCES, lambda m: send_new(m).wait_send())
        each(0, SENTENCES, lambda m: send_old(m).wait_send())

    for k in keep:
        k.wait()


def layers(meta, x, cot, gains, w_qkv, w_out, w_up, w_down, w_cross, picks):
    V, S = pltpu.VMEM, pltpu.SemaphoreType.DMA
    rows16 = V((ROWS, D), BF16)
    rows32 = V((ROWS, D), F32)
    scratch = [
        rows16, rows16, rows16, V((8, D), F32), V((D, 3 * D), BF16), V((D, D), BF16), V((D, FF), BF16), V((FF, D), BF16),
        V((D, 2 * D), BF16), V((D, 2 * D), BF16), V((2, D, D), BF16),
        rows16, V((ROWS, 3 * D), BF16), rows16, V((SENTENCES * HEADS, SEQ, SEQ), BF16), rows32, rows16, rows16,
        V((SENTENCES, 2 * SEQ, D), BF16), V((SENTENCES, 2 * SEQ, D), BF16), V((SENTENCES, 2 * SEQ, 2 * D), BF16), rows16,
        V((SENTENCES * HEADS, 2 * SEQ, SEQ), BF16), rows32, rows16, V((ROWS, FF), BF16), V((ROWS, FF), BF16), rows16, rows16, rows16, rows32,
        V((HALF, D), F32), V((2, D, FF_BLOCK), BF16), V((2, FF_BLOCK, D), BF16),
        S((8,)), S((15,)), S((12,)), S((12,))]
    return pl.pallas_call(
        layers_kernel,
        name="layers",
        out_shape=(
            shape(ROWS, D), shape(ROWS, D, dtype=F32), shape(ROWS, D, dtype=F32), shape(ROWS, D), shape(ROWS, 3 * D), shape(ROWS, D),
            shape(SENTENCES * HEADS, SEQ, SEQ), shape(8, D, dtype=F32), shape(D, FF), shape(FF, D), shape(D, 2 * D), shape(D, 2 * D)),
        in_specs=[IN_SMEM, IN_HBM, IN_HBM, IN_VMEM] + [IN_HBM] * 6,
        out_specs=[IN_HBM] * 7 + [IN_VMEM] + [IN_HBM] * 4,
        scratch_shapes=scratch,
        compiler_params=pltpu.CompilerParams(collective_id=1, has_side_effects=True, vmem_limit_bytes=VMEM_LIMIT),
    )(meta, x, cot, gains, w_qkv, w_out, w_up, w_down, w_cross, picks)


class Copies:
    def __init__(self, send, recv):
        self.send, self.recv, self.count = send, recv, 0

    def make(self, src, dst, device):
        k = self.count
        self.count += 1
        return pltpu.make_async_remote_copy(
            src_ref=src, dst_ref=dst, send_sem=self.send.at[k], recv_sem=self.recv.at[k], device_id=device, device_id_type=MESH)


def add_rows(dst, src, count, step=16):
    def body(i):
        at = block(i, step)
        dst[at] = dst[at] + src[at]

    each(0, count // step, body)


def total_rows(*refs):
    return sum(r.astype(F32) for r in refs)


class RowGroup:
    def __init__(self, copies, mine, theirs, loads, bufs, out, sibling, first, second, across):
        self.copies, self.mine, self.theirs, self.loads, self.out = copies, mine, theirs, loads, out
        self.got, self.a, self.b, self.t, self.a2, self.b2, self.y = bufs
        self.sibling, self.plus, self.minus = sibling, *first
        self.plus2, self.minus2 = second
        self.across = across
        self.core = {r: copies.make(theirs(r), self.got.at[r], sibling) for r in (2, 1, 3, 0)}
        top, low = pl.ds(0, 48), pl.ds(48, 32)
        mk = copies.make
        self.a_p, self.a_m = mk(mine.at[2, top], self.a.at[0, top], self.plus), mk(mine.at[2, low], self.a.at[1, low], self.minus)
        self.b_p, self.b_m = mk(mine.at[1, low], self.b.at[0, low], self.plus), mk(mine.at[3, top], self.b.at[1, top], self.minus)
        self.c_p, self.c_m = mk(mine.at[1, top], self.b.at[0, top], self.plus), mk(mine.at[3, low], self.b.at[1, low], self.minus)
        top, low = pl.ds(0, 16), pl.ds(16, 16)
        t, a2, b2 = self.t, self.a2, self.b2
        self.d_p, self.d_m = mk(t.at[2, top], a2.at[0, top], self.plus2), mk(t.at[2, low], a2.at[1, low], self.minus2)
        self.e_p, self.e_m = mk(t.at[1, low], b2.at[0, low], self.plus2), mk(t.at[3, top], b2.at[1, top], self.minus2)
        self.f_p, self.f_m = mk(t.at[1, top], b2.at[0, top], self.plus2), mk(t.at[3, low], b2.at[1, low], self.minus2)
        self.last = mk(self.y.at[0], self.y.at[1], across)

    def load(self):
        for k in self.loads.values():
            k.start()

    def start(self):
        for k in self.core.values():
            k.start()

    def summed(self, r):
        if r in self.loads:
            self.loads[r].wait()
        self.core[r].wait_recv()
        add_rows(self.mine.at[r], self.got.at[r], 80)

    def first(self):
        self.summed(2)
        self.a_p.start()
        self.a_m.start()
        self.summed(1)
        self.b_p.start()
        self.summed(3)
        self.b_m.start()

    def second(self):
        top, low = pl.ds(0, 48), pl.ds(48, 32)
        self.a_p.wait_recv()
        add_rows(self.mine.at[1, top], self.a.at[0, top], 48)
        self.c_p.start()
        self.a_m.wait_recv()
        add_rows(self.mine.at[3, low], self.a.at[1, low], 32)
        self.c_m.start()
        self.summed(0)

    def third(self):
        for k in (self.b_p, self.b_m, self.c_p, self.c_m):
            k.wait_recv()
        for r in range(4):
            at = pl.ds(20 * r, 20)
            got = total_rows(self.mine[0, at], self.b[0, at], self.b[1, at])
            self.t[r] = jnp.concatenate([got, jnp.zeros((12, got.shape[1]), F32)], axis=0).astype(BF16)
        for k in (self.d_p, self.d_m, self.e_p, self.e_m):
            k.start()

    def fourth(self):
        top, low = pl.ds(0, 16), pl.ds(16, 16)
        self.d_p.wait_recv()
        add_rows(self.t.at[1, top], self.a2.at[0, top], 16)
        self.f_p.start()
        self.d_m.wait_recv()
        add_rows(self.t.at[3, low], self.a2.at[1, low], 16)
        self.f_m.start()

    def fifth(self):
        for k in (self.e_p, self.e_m, self.f_p, self.f_m):
            k.wait_recv()
        got = total_rows(self.t[0], self.b2[0], self.b2[1])
        self.y[0] = got[10:26].astype(BF16)
        self.last.start()
        self.out[...] = got[0:10]

    def sixth(self):
        self.last.wait_recv()
        self.out[...] = self.out[...] + self.y[1, 0:10].astype(F32)

    def drain(self):
        for k in (*self.core.values(), self.a_p, self.a_m, self.b_p, self.b_m, self.c_p, self.c_m,
                  self.d_p, self.d_m, self.e_p, self.e_m, self.f_p, self.f_m, self.last):
            k.wait_send()


class DownGroup:
    def __init__(self, copies, mine, theirs, loads, bufs, out, sibling, first, second, across, x, y):
        self.mine, self.loads, self.out, self.x, self.y_at = mine, loads, out, x, y
        self.got, self.a, self.b, self.a2, self.b2, self.y = bufs
        mk = copies.make
        plus, minus = first
        plus2, minus2 = second
        self.core = {r: mk(theirs(r), self.got.at[r], sibling) for r in (2, 1, 3, 0)}
        top, low = pl.ds(0, 2), pl.ds(2, 2)
        self.a_p, self.a_m = mk(mine.at[2, top], self.a.at[0, top], plus), mk(mine.at[2, low], self.a.at[1, low], minus)
        self.b_p, self.b_m = mk(mine.at[1, low], self.b.at[0, low], plus), mk(mine.at[3, top], self.b.at[1, top], minus)
        self.c_p, self.c_m = mk(mine.at[1, top], self.b.at[0, top], plus), mk(mine.at[3, low], self.b.at[1, low], minus)
        at = lambda r: (x + r) % 4
        self.at = at
        self.d_p, self.d_m = mk(mine.at[0, at(2), 0], self.a2.at[0], plus2), mk(mine.at[0, at(2), 1], self.a2.at[1], minus2)
        self.e_p, self.e_m = mk(mine.at[0, at(1), 1], self.b2.at[0, 1], plus2), mk(mine.at[0, at(3), 0], self.b2.at[1, 0], minus2)
        self.f_p, self.f_m = mk(mine.at[0, at(1), 0], self.b2.at[0, 0], plus2), mk(mine.at[0, at(3), 1], self.b2.at[1, 1], minus2)
        self.last = mk(self.y.at[0], self.y.at[1], across)

    load, start, drain = RowGroup.load, RowGroup.start, RowGroup.drain

    def add(self, dst, src, lo, count):
        def body(i):
            dst[lo + i // 2, i % 2] = dst[lo + i // 2, i % 2] + src[lo + i // 2, i % 2]

        each(0, 2 * count, body)

    def summed(self, r):
        self.loads[r].wait()
        self.core[r].wait_recv()
        self.add(self.mine.at[r], self.got.at[r], 0, 4)

    first = RowGroup.first

    def second(self):
        self.a_p.wait_recv()
        self.add(self.mine.at[1], self.a.at[0], 0, 2)
        self.c_p.start()
        self.a_m.wait_recv()
        self.add(self.mine.at[3], self.a.at[1], 2, 2)
        self.c_m.start()
        self.summed(0)

    def third(self):
        for k in (self.b_p, self.b_m, self.c_p, self.c_m):
            k.wait_recv()

        def body(i):
            p, q = i // 2, i % 2
            self.mine[0, p, q] = total_rows(self.mine[0, p, q], self.b[0, p, q], self.b[1, p, q]).astype(BF16)

        each(0, 8, body)
        for k in (self.d_p, self.d_m, self.e_p, self.e_m):
            k.start()

    def fourth(self):
        self.d_p.wait_recv()
        self.mine[0, self.at(1), 0] = self.mine[0, self.at(1), 0] + self.a2[0]
        self.f_p.start()
        self.d_m.wait_recv()
        self.mine[0, self.at(3), 1] = self.mine[0, self.at(3), 1] + self.a2[1]
        self.f_m.start()

    def fifth(self):
        for k in (self.e_p, self.e_m, self.f_p, self.f_m):
            k.wait_recv()
        full = lambda q: total_rows(self.mine[0, self.x, q], self.b2[0, q], self.b2[1, q])
        self.y[0] = full(1 - self.y_at).astype(BF16)
        self.last.start()
        self.out[...] = full(self.y_at)

    def sixth(self):
        self.last.wait_recv()
        self.out[...] = self.out[...] + self.y[1].astype(F32)


GAIN_COLS = 128
CROSS_ROWS = 16


def gradients_kernel(meta, digits, x_hbm, gain_ref, wqkv_hbm, wout_hbm, picks_hbm, dx_hbm, extra_hbm, a_hbm, qkv_hbm, o_hbm, p_hbm,
                     gsum_in, dup_hbm, ddn_hbm, dcross_hbm, dwc_hbm,
                     dstream_hbm, up_out, down_out, qkv_out, rest_out, cross_out, *scratch):
    (x, wqkv, wout, picks, dx, extra, a, qkv, o, p, dbr, d_o, dqkv, tmp, gpad, fx2, fz2, wc_out, wc_send,
     up_mine, down_mine, cross_mine, wc_mine, up_bufs, down_bufs, cross_bufs, wc_bufs, x2_bufs, z2_bufs,
     load_sem, group_sem, out_sem, send_sem, recv_sem) = scratch
    section = lax.axis_index("section")
    px, py, pz, core = place()
    partner = {"section": 1 - section, "dp": lax.axis_index("dp")}
    own = {"section": section}
    sibling = {**own, **device_at(px, py, pz, 1 - core)}
    x_ring = [{**own, **device_at((px + r) % 4, py, pz, core)} for r in (1, 3)]
    z_ring = [{**own, **device_at(px, py, (pz + r) % 4, core)} for r in (1, 3)]
    across = {**own, **device_at(px, 1 - py, pz, core)}
    barrier = pltpu.get_barrier_semaphore()
    for d in (sibling, *x_ring, *z_ring, across, partner):
        pl.semaphore_signal(barrier, inc=1, device_id=d, device_id_type=MESH)

    copies = Copies(send_sem, recv_sem)

    def local(k, src, dst):
        return pltpu.make_async_copy(src, dst, group_sem.at[k])

    def from_hbm(at, hbm, mine):
        return {r: local(at + r, hbm.at[0, r], mine.at[r]) for r in (2, 1, 3, 0)}

    up = RowGroup(copies, up_mine, lambda r: dup_hbm.at[1, r], from_hbm(0, dup_hbm, up_mine), up_bufs, up_out, sibling, x_ring, z_ring, across)
    down = DownGroup(
        copies, down_mine, lambda r: ddn_hbm.at[:, :, (pz + r) % 4, 1 - core],
        {r: local(4 + r, ddn_hbm.at[:, :, (pz + r) % 4, core], down_mine.at[r]) for r in (2, 1, 3, 0)},
        down_bufs, down_out, sibling, z_ring, x_ring, across, px, py)
    cross = RowGroup(copies, cross_mine, lambda r: dcross_hbm.at[1, r], from_hbm(8, dcross_hbm, cross_mine), cross_bufs, cross_out, sibling, x_ring, z_ring, across)
    encoded = RowGroup(copies, wc_mine, lambda r: dwc_hbm.at[1, r], from_hbm(12, dwc_hbm, wc_mine), wc_bufs, wc_out, sibling, z_ring, x_ring, across)
    late_x = RowGroup(copies, fx2, lambda r: fx2.at[4 + r], {}, x2_bufs, qkv_out, sibling, x_ring, z_ring, across)
    late_z = RowGroup(copies, fz2, lambda r: fz2.at[4 + r], {}, z2_bufs, rest_out, sibling, z_ring, x_ring, across)
    send_cross = copies.make(wc_send.at[0], wc_send.at[1], partner)

    def decoder(*steps):
        @pl.when(section == 1)
        def _():
            for step in steps:
                step()

    gets = [pltpu.make_async_copy(src, dst, load_sem.at[i]) for i, (src, dst) in enumerate((
        (dx_hbm, dx), (wout_hbm, wout), (p_hbm, p), (qkv_hbm, qkv), (o_hbm, o), (a_hbm, a), (picks_hbm, picks), (wqkv_hbm, wqkv), (x_hbm, x), (extra_hbm, extra)))]
    get_dx, get_out, get_p, get_qkv, get_o, get_a, get_picks, get_wqkv, get_x, get_extra = gets
    get_dx.start()
    get_out.start()
    up.load()
    down.load()
    decoder(cross.load, encoded.load)
    for k in gets[2:]:
        k.start()
    pl.semaphore_wait(barrier, 7)
    up.start()
    down.start()
    decoder(cross.start, encoded.start)

    gain = gain_ref[0:1]
    get_dx.wait()

    def branch(m):
        s = Sentence(meta, m)
        dbr[block(m)] = (dx[block(m)] * s.mask * s.rows()).astype(BF16)

    each(0, SENTENCES, branch)
    get_out.wait()
    tmp[...] = mm_nt(dbr[...], wout[...])
    up.first()
    down.first()
    get_p.wait()
    get_qkv.wait()

    def attention(m):
        s = Sentence(meta, m)
        rows = block(m)
        d_o[rows] = (tmp[rows] * s.heads).astype(BF16)
        dq, dk, dv = attend_back(
            lambda h: d_o[rows, slice(*window(h))],
            lambda h: qkv[rows, slice(*window(h))],
            lambda h: qkv[rows, D + window(h)[0] : D + window(h)[1]],
            lambda h: qkv[rows, 2 * D + window(h)[0] : 2 * D + window(h)[1]],
            lambda h: p[m * HEADS + h])
        dqkv[rows, 0:D] = dq
        dqkv[rows, D : 2 * D] = dk
        dqkv[rows, 2 * D : 3 * D] = dv

    each(0, SENTENCES, attention)
    get_a.wait()
    get_picks.wait()
    turn = lambda k, value: mm_nt(picks[k], value).astype(BF16)
    fx2[...] = mm(turn(0, a[...]), dqkv[:, 0 : 2 * D]).astype(BF16).reshape(fx2.shape)
    late_x.start()
    decoder(cross.first, encoded.first)
    up.second()
    down.second()
    get_wqkv.wait()
    tmp[...] = mm_nt(dqkv[...], wqkv[...])
    get_x.wait()
    gpad[...] = jnp.zeros_like(gpad)
    get_extra.wait()

    @pl.when(section == 1)
    def _():
        extra[...] = jnp.zeros_like(extra)

    def finish(m):
        s = Sentence(meta, m)
        rows = block(m)
        n, r = normalize(x[rows].astype(F32), s.mask, s.inv)
        dy = tmp[rows]
        gpad[0:1] += jnp.sum(dy * n, 0, keepdims=True)
        d = dx[rows] + normalize_back(dy * gain, n, r, s.mask, s.inv) + extra[rows]
        d_o[rows] = d.astype(BF16)

    get_o.wait()
    zt = turn(1, o[...])
    fz2[:, :, 0:D] = mm(zt, dbr[...]).astype(BF16).reshape(8, 80, D)
    fz2[:, :, D : 2 * D] = mm(turn(1, a[...]), dqkv[:, 2 * D : 3 * D]).astype(BF16).reshape(8, 80, D)
    each(0, SENTENCES, finish)
    put = pltpu.make_async_copy(d_o, dstream_hbm, out_sem.at[0])
    put.start()
    gpad[1:3] = gsum_in[1:3]
    gains_t = turn(1, gpad[...].astype(BF16)).astype(F32) + digits[0:1]
    fz2[:, :, 2 * D : 2 * D + GAIN_COLS] = gains_t.astype(BF16).reshape(8, 80, GAIN_COLS)
    late_z.start()
    decoder(cross.second, encoded.second)
    late_x.first()
    late_z.first()
    up.third()
    down.third()
    decoder(cross.third, encoded.third)
    late_x.second()
    late_z.second()
    up.fourth()
    down.fourth()
    decoder(cross.fourth, encoded.fourth)
    late_x.third()
    late_z.third()
    up.fifth()
    down.fifth()
    decoder(cross.fifth, encoded.fifth)
    late_x.fourth()
    late_z.fourth()
    up.sixth()
    down.sixth()

    @pl.when(section == 1)
    def _():
        cross.sixth()
        encoded.sixth()
        wc_send[0, 0:10] = wc_out[...]
        send_cross.start()

    late_x.fifth()
    late_z.fifth()
    late_x.sixth()
    late_z.sixth()

    @pl.when(section == 0)
    def _():
        send_cross.wait_recv()
        cross_out[...] = wc_send[1, 0:10]

    for group in (up, down, late_x, late_z):
        group.drain()
    decoder(cross.drain, encoded.drain, send_cross.wait_send)
    put.wait()


def row_bufs(n):
    V = pltpu.VMEM
    return [V((4, 80, n), BF16), V((2, 80, n), BF16), V((2, 80, n), BF16), V((4, 32, n), BF16), V((2, 32, n), BF16), V((2, 32, n), BF16), V((2, 16, n), BF16)]


def gradients(meta, digits, x, gains, w_qkv, w_out, picks, dx, extra, a, qkv, o, p, gsum, dup, ddn, dcross, dwc):
    V, S = pltpu.VMEM, pltpu.SemaphoreType.DMA
    rows16, rows32 = V((ROWS, D), BF16), V((ROWS, D), F32)
    late = 2 * D + GAIN_COLS
    scratch = [
        rows16, V((D, 3 * D), BF16), V((D, D), BF16), V((2, D, D), BF16), rows32, rows32, rows16, V((ROWS, 3 * D), BF16), rows16,
        V((SENTENCES * HEADS, SEQ, SEQ), BF16), rows16, rows16, V((ROWS, 3 * D), BF16), rows32, V((GAIN_COLS, D), F32),
        V((8, 80, 2 * D), BF16), V((8, 80, late), BF16), V((10, 2 * D), F32), V((2, CROSS_ROWS, 2 * D), F32),
        V((4, 80, FF), BF16), V((4, 4, 2, 48, D), BF16), V((4, 80, 2 * D), BF16), V((4, 80, 2 * D), BF16),
        row_bufs(FF),
        [V((4, 4, 2, 48, D), BF16), V((2, 4, 2, 48, D), BF16), V((2, 4, 2, 48, D), BF16), V((2, 48, D), BF16), V((2, 2, 48, D), BF16), V((2, 48, D), BF16)],
        row_bufs(2 * D), row_bufs(2 * D), row_bufs(2 * D), row_bufs(late),
        S((10,)), S((16,)), S((1,)), S((103,)), S((103,))]
    f32 = functools.partial(shape, dtype=F32)
    return pl.pallas_call(
        gradients_kernel,
        name="gradients",
        out_shape=(shape(ROWS, D), f32(10, FF), f32(48, D), f32(10, 2 * D), f32(10, late), f32(10, 2 * D)),
        in_specs=[IN_SMEM, IN_VMEM, IN_HBM, IN_VMEM] + [IN_HBM] * 9 + [IN_VMEM] + [IN_HBM] * 4,
        out_specs=[IN_HBM] + [IN_VMEM] * 5,
        scratch_shapes=scratch,
        compiler_params=pltpu.CompilerParams(collective_id=0, has_side_effects=True, vmem_limit_bytes=VMEM_LIMIT),
    )(meta, digits, x, gains, w_qkv, w_out, picks, dx, extra, a, qkv, o, p, gsum,
      dup.reshape(2, 4, 80, FF), ddn.reshape(4, 2, 4, 2, 48, D), dcross.reshape(2, 4, 80, 2 * D), dwc.reshape(2, 4, 80, 2 * D))


DIGITS = 5


def shards(stream, cotangent, lengths, pieces, configs, gains, attn_qkv, attn_out, ffn_up, ffn_down, cross_proj):
    later = lax.axis_index("section").astype(jnp.int32)
    x = stream.reshape(ROWS, D)
    cot = cotangent.reshape(ROWS, D)
    onehot = (pieces == jnp.arange(configs.shape[0], dtype=jnp.int32)[None, :]).astype(jnp.int32)
    chosen = jnp.sum(onehot[:, :, None] * configs[None], axis=1)
    lens = lengths[:, :, 0]
    own = jnp.where(later == 1, lens[1], lens[0])
    meta = jnp.stack(
        [chosen[:, 0], chosen[:, 1] * HEAD_DIM, chosen[:, 2], chosen[:, 3] * SEQ, own, lens[0], jnp.broadcast_to(later, own.shape), own], axis=1)
    counts = jnp.stack([
        jnp.sum(own), jnp.sum(own * (chosen[:, 1] == HEADS)), jnp.sum(own * (chosen[:, 2] > FF_BLOCK)), jnp.sum(own * (chosen[:, 2] > 2 * FF_BLOCK))])
    powers = 4 ** jnp.arange(DIGITS, dtype=jnp.int32)
    digits = (counts[:, None] // powers[None, :]) % 4
    digits = jnp.pad(digits.reshape(1, -1).astype(F32), ((0, 7), (3, GAIN_COLS - 3 - 4 * DIGITS)))
    feature = jnp.arange(D, dtype=jnp.int32)
    picks = jnp.stack([(relative_order(k)[:, None] == feature[None, :]).astype(BF16) for k in ("x", "z")])
    gains_in = jnp.pad(gains[0].astype(F32), ((0, 5), (0, 0)))
    w = (attn_qkv[0], attn_out[0], ffn_up[0], ffn_down[0], cross_proj[0])
    layer_out, dx, extra, a, qkv, o, p, gsum, dup, ddn, dcross, dwc = layers(meta, x, cot, gains_in, *w, picks)
    dstream, up, down, qkv_x, rest, cross = gradients(
        meta, digits, x, gains_in, w[0], w[1], picks, dx, extra, a, qkv, o, p, gsum, dup, ddn, dcross, dwc)

    sums = rest[0, 2 * D + 3 : 2 * D + 3 + 4 * DIGITS].reshape(4, DIGITS)
    totals = jnp.sum(sums * powers[None, :].astype(F32), axis=1)
    devices = lax.axis_size("dp")
    tokens_all = float(ROWS * devices)
    rates = tokens_all / (totals + float(ROWS * devices // 8))
    me = lax.axis_index("dp")
    qkv_cols = jnp.arange(3 * D, dtype=jnp.int32) % D // HEAD_DIM >= HEADS // 2
    out_count = D // devices
    out_rows = (me * out_count + jnp.arange(out_count, dtype=jnp.int32)) // HEAD_DIM >= HEADS // 2
    up_block = jnp.arange(FF, dtype=jnp.int32) // FF_BLOCK
    by_block = lambda k: jnp.where(k == 0, rates[0], jnp.where(k == 1, rates[2], rates[3]))
    down_count = FF // devices
    down_block = (me * down_count + jnp.arange(down_count, dtype=jnp.int32)) // FF_BLOCK
    qkv_grad = jnp.concatenate([qkv_x, rest[:, D : 2 * D]], axis=1) * jnp.where(qkv_cols, rates[1], rates[0])[None, :]
    out_grad = rest[:, 0:D] * jnp.where(out_rows, rates[1], rates[0])[:, None]
    up_grad = up * by_block(up_block)[None, :]
    down_grad = down * by_block(down_block)[:, None]
    gain_grad = rest[:, 2 * D : 2 * D + 3].T
    return (layer_out.reshape(stream.shape), dstream.reshape(stream.shape), gain_grad[None], qkv_grad[None], out_grad[None],
            up_grad[None], down_grad[None], cross[None])


def solution(mesh):
    in_specs = (
        P("section", None, "dp", None, None),
        P("section", None, "dp", None, None),
        P(None, None, "dp"),
        P(None, "dp"),
        P(),
        P("section", None, None),
        P("section", None, None),
        P("section", None, None),
        P("section", None, None),
        P("section", None, None),
        P("section", None, None),
    )
    out_specs = (
        P("section", None, "dp", None, None),
        P("section", None, "dp", None, None),
        P("section", None, "dp"),
        P("section", "dp", None),
        P("section", "dp", None),
        P("section", "dp", None),
        P("section", "dp", None),
        P("section", "dp", None),
    )
    return jax.shard_map(shards, mesh=mesh, in_specs=in_specs, out_specs=out_specs, check_vma=False)
```

time: 1180 us -> 188 us (0.16)
  waiting for transfers between devices: 363 us -> 0 us
  local copies, waits for them, and re-layouts: 318 us -> 9.09 us
  matrix products: 279 us -> 0 us
  Pallas kernels: 0 us -> 153 us
  other arithmetic: 107 us -> 21.3 us
  loops' own time: 53.6 us -> 0 us
  starting transfers between devices: 28.5 us -> 0 us
  between operations: 17.7 us -> 1.19 us
    reduce_scatter x1 -> x0, waiting for transfers between devices: 315 us -> none  [sum_packed(): lax.psum_scatter(lines, axis, tiled=True).reshape(-1)]
    dot_general x104 -> x0, matrix products: 275 us -> none  [the longest x28 91.7 us: project(): jnp.einsum('ayb,bc->ayc', barrier_operand, weight_matrix, preferred_eleme...]
    pallas_call x0 -> x2, Pallas kernels: none -> 153 us  [the longest x1 89.1 us: layers(): pl.pallas_call(layers_kernel, name='layers', out_shape=(shape(ROWS, D), s...]
    cond x261 -> x0, local copies, waits for them, and re-layouts: 82.7 us -> none
    unnamed x93 -> x13, local copies, waits for them, and re-layouts: 75.8 us -> 5.13 us
    another operation x16 -> x0, loops' own time: 53.6 us -> none  [the longest x4 29.1 us: shards(): first = lax.cond(later, late_step, early_step)]
    another operation x22 -> x3, local copies, waits for them, and re-layouts: 46.6 us -> 0.76 us  [the longest x2 0.68 us: shards(): jnp.stack([chosen[:, 0], chosen[:, 1] * HEAD_DIM, chosen[:, 2], chosen[:,...]
    ppermute x8 -> x0, waiting for transfers between devices: 38.6 us -> none  [passed_along(): lax.ppermute(value, axis, [(source, source + steps) for source in range(f...]
  transfers between devices with their start and end apart: 10 -> 0, of which waited for: 5 -> 0; matrix products, arithmetic and copies ran while one was open for 32% -> 0% of each run, Pallas kernels for 0% -> 0%
where the time goes in v2:
time: 188 us; the launch traced here: 184 us
  Pallas kernels  153 us (81%)
  other arithmetic  21.3 us (11%)
  local copies, waits for them, and re-layouts  9.09 us (5%)
    pallas_call x1, Pallas kernels, layers(): pl.pallas_call(layers_kernel, name='layers', out_shape=(shape(ROWS, D), s...  89.1 us
    pallas_call x1, Pallas kernels, gradients(): pl.pallas_call(gradients_kernel, name='gradients', out_shape=(shape(ROWS,...  63.6 us
    unnamed x13, local copies, waits for them, and re-layouts  5.13 us
    select_n x2, other arithmetic, shards(): jnp.where(k == 0, rates[0], jnp.where(k == 1, rates[2], rates[3]))  3.89 us

profile of v2, /device:TPU:0, one launch (start us, length us, event | category | flops | bytes accessed | tf_op | source)
XLA Modules:
  0.0 184.3 jit_solution(13894578658981358651)
XLA Ops:
  0.6 0.7 fusion.50
  1.4 0.8 multiply_reduce_fusion
  2.1 1.3 fusion.61
  4.4 1.3 pad_convert_fusion.gain_ref
  6.3 1.5 add_convert_fusion.picks_hbm
  7.8 89.1 %layers.1 = (bf16[512,640]{1,0:T(8,128)(2,1)}, f32[512,640]{1,0:T(8,128)}, f32[512,640]{1,0:T(8,128)}, bf16[512,640]{1,0:T(8,128)(2,1)}, bf16[512,1920]{1,0:T(8,...) custom-call(s32[4,8]{1,0:T(4,128)} %stack.29.meta, ...), custom_call_target="tpu_custom_call" | custom-call | tf_op jit(solution)/shard_map/layers/pallas_call | solution.py:556
  97.2 0.7 fusion.55
  97.9 2.7 %fusion.60 = (s32[4]{0:T(128)S(1)}, s32[4]{0:T(128)S(1)}) fusion(s32[1]{0:T(128)} %bitcast.17, s32[1]{0:T(128)} %bitcast.16, s32[1]{0:T(128)} %bitcast.15, s32[1]{0:T(128)} %bitcast.13), kind=kLoop, calls=%fused_computation.161 | loop fusion | flops 16 | bytes 48 | tf_op jit(solution)/shard_map/jit(floor_divide)/sign | solution.py:979
  101.8 63.6 %gradients.1 = (bf16[512,640]{1,0:T(8,128)(2,1)}, f32[10,3072]{1,0:T(8,128)}, f32[48,640]{1,0:T(8,128)}, f32[10,1280]{1,0:T(8,128)}, f32[10,1408]{1,0:T(8,128)}, /*index=5*/f32[10,1280]{1,0:T(8,128)}) custom-call(s32[4,8]{1,0:T(4,128)} %stack.29.meta, f32[8,128]{1,0:T(8,128)} %pad.12.digits, bf16[512,640]{1,0:T(8,128)(2,1)} %bitcast.64, ...), custom_call_target="tpu_custom_call" | custom-call | tf_op jit(solution)/shard_map/gradients/pallas_call | solution.py:951
  165.4 0.8 slice_bitcast_fusion.1
  166.9 0.8 slice_reduce_fusion
  168.5 1.3 compare_select_fusion.4
  169.8 0.9 multiply_bitcast_fusion.2
  170.7 1.3 fusion.8
  172.0 0.9 maximum_multiply_fusion
  172.9 0.7 copy.37
  174.2 1.9 %select_select_fusion = f32[3072]{0:T(1024)S(1)} fusion(f32[]{:T(128)} %bitcast.32, f32[]{:T(128)} %bitcast.31, f32[]{:T(128)} %bitcast.29), kind=kLoop, calls=%fused_computation.16 | loop fusion | flops 36864 | bytes 12300 | tf_op jit(solution)/shard_map/jit(_where)/select_n | solution.py:999
  176.2 0.9 multiply_bitcast_fusion
  177.1 0.8 copy.39
  177.9 1.9 %compare_select_fusion.3 = f32[48]{0:T(128)S(1)} fusion(f32[]{:T(128)} %bitcast.32, f32[]{:T(128)} %bitcast.31, f32[]{:T(128)} %bitcast.29, s32[]{:T(128)S(6)} %mul.230), kind=kLoop, calls=%fused_computation.120 | loop fusion | flops 960 | bytes 208 | tf_op jit(solution)/shard_map/jit(_where)/select_n | solution.py:999
  179.9 1.6 multiply_bitcast_fusion.1
  181.5 0.7 copy.40
  182.2 0.8 copy.45
  183.0 0.8 copy.46
  (29 shorter events, 5.2 us)
Async XLA Ops:
  165.4 16.1 %copy-start.2 = (f32[10,1280]{1,0:T(8,128)S(1)}, f32[10,1280]{1,0:T(8,128)}, u32[]{:S(2)}) copy-start(f32[10,1280]{1,0:T(8,128)} %get-tuple-element.43) | copy-start | bytes 153604
  165.4 16.8 %copy-start = (bf16[512,640]{1,0:T(8,128)(2,1)S(1)}, bf16[512,640]{1,0:T(8,128)(2,1)}, u32[]{:S(2)}) copy-start(bf16[512,640]{1,0:T(8,128)(2,1)} %get-tuple-element.26) | copy-start | bytes 1966084
  165.4 17.6 %copy-start.1 = (bf16[512,640]{1,0:T(8,128)(2,1)S(1)}, bf16[512,640]{1,0:T(8,128)(2,1)}, u32[]{:S(2)}) copy-start(bf16[512,640]{1,0:T(8,128)(2,1)} %get-tuple-element.38) | copy-start | bytes 1966084
